TPU v7x, 256 devices: a whole 4x4x8 slice. The times are simulated.
256 devices in a mesh: dp: 16 (over z, core), tensor: 16 (over x, y).
Axes of the slice: x: 4, y: 4, z: 8, core: 2. Of those that a mesh axis runs over, the one named last changes fastest.
Arguments:
- qkv_img: bfloat16 [16, 1024, 3, 2432], P('dp', 'tensor'), may hold values from -16 to 16
- tan_img: bfloat16 [16, 1024, 3, 2432], P('dp', 'tensor'), may hold values from -96 to 96
- txt_kv: bfloat16 [16, 48, 333, 256], P('dp', 'tensor'), may hold values from -5 to 5
- head_table: int32 [16, 3], replicated, may hold values from -1 to 37, as said below
- out_weight: bfloat16 [3072, 2432], P('tensor'), may hold values from -2.390625 to 2.390625
- cotangent: bfloat16 [16, 1024, 2432], P('dp', 'tensor'), may hold values from -6 to 6
Outputs:
- image_out: bfloat16 [16, 1024, 2432], P('dp', 'tensor')
- tangent_out: bfloat16 [16, 1024, 2432], P('dp', 'tensor')
- weight_grad: float32 [3072, 2432], P('tensor')
Inputs may be any that keep to these rules, and one draw needn't show every extreme that they name: `head_table`: each of the 38 heads stands in exactly one slot and the other slots hold -1; some index of tensor has all 3 slots filled.
All inputs are finite; a program needn't handle non-finite values.
Results may differ from a plain program's by a relative error of at most 0.023.
Values may be sent and summed in bfloat16 or wider, within the bound.
A program may use at most 128 MiB of HBM per device.

v0:
```python
import jax
import jax.numpy as jnp
from jax import lax
from jax.sharding import PartitionSpec as P


def attend(slot_data, text_rows, filled):
    head_size = text_rows.shape[1] // 4
    score_scale = head_size ** (-0.5)
    queries = slot_data[:, :head_size]
    tangent_queries = slot_data[:, 3 * head_size : 4 * head_size]
    key_rows = jnp.concatenate(
        [slot_data[:, head_size : 2 * head_size], text_rows[:, :head_size]], 0
    )
    value_rows = jnp.concatenate(
        [slot_data[:, 2 * head_size : 3 * head_size], text_rows[:, head_size : 2 * head_size]], 0
    )
    tangent_keys = jnp.concatenate(
        [slot_data[:, 4 * head_size : 5 * head_size], text_rows[:, 2 * head_size : 3 * head_size]],
        0,
    )
    tangent_values = jnp.concatenate(
        [slot_data[:, 5 * head_size :], text_rows[:, 3 * head_size :]], 0
    )
    scores = jnp.dot(queries, key_rows.T, preferred_element_type=jnp.float32) * score_scale
    query_pair = jnp.concatenate([tangent_queries, queries], 1)
    key_pair = jnp.concatenate([key_rows, tangent_keys], 1)
    tangent_scores = (
        jnp.dot(query_pair, key_pair.T, preferred_element_type=jnp.float32) * score_scale
    )
    row_max = jnp.max(scores, axis=1, keepdims=True)
    expanded = jnp.exp(scores - row_max)
    probs = expanded / jnp.sum(expanded, axis=1, keepdims=True)
    tangent_probs = probs * (
        tangent_scores - jnp.sum(probs * tangent_scores, axis=1, keepdims=True)
    )
    probs_low = probs.astype(jnp.bfloat16)
    tangent_low = tangent_probs.astype(jnp.bfloat16)
    attn_out = jnp.dot(probs_low, value_rows, preferred_element_type=jnp.float32)
    weight_pair = jnp.concatenate([tangent_low, probs_low], 1)
    value_pair = jnp.concatenate([value_rows, tangent_values], 0)
    attn_tan = jnp.dot(weight_pair, value_pair, preferred_element_type=jnp.float32)
    joined = jnp.concatenate([attn_out, attn_tan], 1)
    return jnp.where(filled, joined, jnp.zeros_like(joined)).astype(jnp.bfloat16)


def on_device(qkv_img, tan_img, txt_kv, head_table, out_weight, cotangent):
    tensor_size = lax.axis_size("tensor")
    own_index = lax.axis_index("tensor")
    img_dev = qkv_img.shape[1]
    model_width = qkv_img.shape[3]
    head_size = txt_kv.shape[3] // 4
    slot_count = head_table.shape[1]
    head_count = model_width // head_size
    stacked = jnp.concatenate([qkv_img[0], tan_img[0]], 1).reshape(
        img_dev, 6, head_count, head_size
    )
    chosen = jnp.take(stacked, jnp.maximum(head_table, 0).reshape(-1), axis=2)
    outgoing = chosen.reshape(img_dev, 6, tensor_size, slot_count, head_size)
    outgoing = outgoing.transpose(2, 0, 3, 1, 4).reshape(
        tensor_size, img_dev, slot_count, 6 * head_size
    )
    arrived = lax.all_to_all(outgoing, "tensor", split_axis=0, concat_axis=1, tiled=True)[0]
    live_row = lax.dynamic_index_in_dim(head_table, own_index, 0, keepdims=False) >= 0

    def one_slot(slot_inputs):
        slot_data, text_rows, slot_filled = slot_inputs
        return attend(slot_data, text_rows, slot_filled)

    per_slot = lax.map(one_slot, (jnp.moveaxis(arrived, 1, 0), txt_kv[0], live_row))
    combined = jnp.moveaxis(per_slot, 0, 1)
    total_rows = combined.shape[0]
    attn_prim = combined[:, :, :head_size].reshape(total_rows, slot_count * head_size)
    attn_tang = combined[:, :, head_size:].reshape(total_rows, slot_count * head_size)
    outputs_pair = jnp.stack([attn_prim, attn_tang], 1)
    projected = lax.psum_scatter(
        jnp.einsum("rcj,jd->rcd", outputs_pair, out_weight, preferred_element_type=jnp.float32),
        "tensor",
        scatter_dimension=0,
        tiled=True,
    )
    image_out = projected[:, 0].astype(jnp.bfloat16)
    tan_sum = projected[:, 1]
    squares = lax.psum(jnp.sum(tan_sum * tan_sum), "tensor")
    root_mean = jnp.sqrt(squares / (img_dev * tensor_size * model_width))
    tangent_out = (tan_sum / (root_mean + 0.1)).astype(jnp.bfloat16)
    upstream = (cotangent[0].astype(jnp.float32) - tangent_out.astype(jnp.float32)).astype(
        jnp.bfloat16
    )
    partial_grad = lax.dot_general(
        attn_prim,
        lax.all_gather(upstream, "tensor", axis=0, tiled=True),
        (((0,), (0,)), ((), ())),
        preferred_element_type=jnp.float32,
    )
    weight_grad = lax.psum(partial_grad.astype(jnp.bfloat16), "dp").astype(
        jnp.float32
    ) / lax.axis_size("dp")
    return (image_out[None], tangent_out[None], weight_grad)


def solution(mesh):
    return jax.shard_map(
        on_device,
        mesh=mesh,
        in_specs=(
            P("dp", "tensor", None, None),
            P("dp", "tensor", None, None),
            P("dp", "tensor", None, None),
            P(),
            P("tensor", None),
            P("dp", "tensor", None),
        ),
        out_specs=(P("dp", "tensor", None), P("dp", "tensor", None), P("tensor", None)),
        check_vma=False,
    )
```

profile of v0, /device:TPU:1, one launch (start us, length us, event | category | flops | bytes accessed | tf_op | source)
XLA Modules:
  0.0 504.0 jit_solution(3466433022178943749)
XLA Ops:
  8.9 2.9 concatenate.44
  11.8 1.7 copy.18
  13.5 3.1 concatenate.45
  17.1 1.0 copy-done.1
  18.1 2.6 pad_maximum_fusion
  20.7 5.5 %gather_fusion = bf16[48,64,6,64]{3,1,2,0:T(8,128)(2,1)} fusion(bf16[64,6,38,64]{3,0,2,1:T(8,128)(2,1)} %pad_maximum_fusion, s32[1024]{0:T(1024)S(1)} %pad_clamp_fusion), kind=kCustom, calls=%fused_computation | custom fusion | bytes 4718784 | tf_op jit(solution)/shard_map/jit(_take)/gather | solution.py:58
  26.2 3.4 copy.21
  30.1 12.2 %copy.22 = bf16[16,64,3,6,64]{4,3,1,2,0:T(8,128)(2,1)} copy(bf16[16,64,3,6,64]{4,1,2,0,3:T(8,128)(2,1)S(1)} %select_bitcast_fusion) | data formatting | bytes 4718592 | tf_op jit(solution)/shard_map/transpose | solution.py:60
  42.3 8.8 %reshape.134 = bf16[16,64,3,384]{3,1,2,0:T(8,128)(2,1)} reshape(bf16[16,64,3,6,64]{4,3,1,2,0:T(8,128)(2,1)} %copy.22) | data formatting | bytes 4718592 | tf_op jit(solution)/shard_map/reshape | solution.py:60
  51.0 7.6 %all-to-all-start = ((bf16[16,64,3,384]{3,1,2,0:T(8,128)(2,1)}), bf16[16,64,3,384]{3,1,2,0:T(8,128)(2,1)S(1)}, u32[]{:S(2)}, u32[]{:S(2)}) async-start(bf16[16,64,3,384]{3,1,2,0:T(8,128)(2,1)} %reshape.134), calls=%async_computation | async-start | bytes 4718592 | tf_op jit(solution)/shard_map/all_to_all | solution.py:63
  58.9 31.4 %all-to-all-done = bf16[16,64,3,384]{3,1,2,0:T(8,128)(2,1)S(1)} async-done(((bf16[16,64,3,384]{3,1,2,0:T(8,128)(2,1)}), bf16[16,64,3,384]{3,1,2,0:T(8,128)(2,1)S(1)}, u32[]{:S(2)}, u32[]{:S(2)}) %all-to-all-start) | async-done | bytes 2359328 | tf_op jit(solution)/shard_map/all_to_all | solution.py:63
  90.3 1.7 copy.23
  92.0 45.1 %while.10 = (s32[]{:T(128)}, bf16[3,1024,128]{1,2,0:T(8,128)(2,1)}, pred[3]{0:T(512)(128)(4,1)S(1)}, bf16[3,1024,384]{2,1,0:T(8,128)(2,1)}, bf16[3,333,256]{2,1,0:T(8,128)(2,1)}, /*index=5*/s32[]{:T(128)}) while((s32[]{:T(128)}, bf16[3,1024,128]{1,2,0:T(8,128)(2,1)}, pred[3]{0:T(512)(128)(4,1)S(1)}, bf16[3,1024,384]{2,1,0:T(8,128)(2,1)}, ...), condition=%wide.region_4.5_spmd, body=%wide.region_0.4_spmd.sunk | while | flops 1107967488 | bytes 55905588 | solution.py:70
  93.7 1.2 dynamic-slice_bitcast_fusion.4
  95.0 1.2 fusion.66
  96.1 1.4 concatenate.48
  98.5 1.0 fusion.68
  99.6 1.8 multiply_reduce_fusion.6
  101.4 1.9 multiply_convert_fusion.2
  104.0 1.7 fusion.69
  105.7 1.4 fusion.70
  108.8 1.2 dynamic-slice_bitcast_fusion.4
  110.0 1.2 fusion.66
  111.2 1.4 concatenate.48
  113.5 1.0 fusion.68
  114.6 1.8 multiply_reduce_fusion.6
  116.4 1.9 multiply_convert_fusion.2
  119.1 1.7 fusion.69
  120.7 1.4 fusion.70
  123.8 1.2 dynamic-slice_bitcast_fusion.4
  125.1 1.2 fusion.66
  126.2 1.4 concatenate.48
  129.6 1.8 multiply_reduce_fusion.6
  131.5 1.9 multiply_convert_fusion.2
  134.1 1.7 fusion.69
  135.8 1.4 fusion.70
  137.2 1.2 fusion.48
  138.4 8.3 %fusion.35 = f32[1024,2,2432]{2,0,1:T(8,128)} fusion(bf16[192,2432]{1,0:T(8,128)(2,1)S(1)} %copy-done, bf16[1024,1,192]{0,2,1:T(8,128)(2,1)S(1)} %bitcast.69, bf16[1024,1,192]{0,2,1:T(8,128)(2,1)S(1)} %bitcast.67), kind=kOutput, calls=%fused_computation.46 | convolution fusion | flops 1912995840 | bytes 21643264 | tf_op jit(solution)/shard_map/rcj,jd->rcd/dot_general | solution.py:77
  146.8 133.4 %reduce-scatter.2.cloned.1.call-done = f32[64,2,2432]{2,0,1:T(8,128)} async-done(((f32[1024,2,2432]{2,0,1:T(8,128)}), f32[64,2,2432]{2,0,1:T(8,128)}) %reduce-scatter.2.cloned.1.call-update) | async-done | bytes 1245200 | tf_op jit(solution)/shard_map/reduce_scatter | solution.py:76
  280.2 1.8 multiply_reduce_fusion.2
  282.0 32.1 %psum.14 = f32[]{:T(128)} all-reduce(f32[]{:T(128)} %multiply_reduce_fusion.2), channel_id=1, replica_groups=mesh['dp'=16,'tensor'=16] {'tensor'}, use_global_device_ids=true, to_apply=%region_7.8 | all-reduce | flops 1 | bytes 8 | tf_op jit(solution)/shard_map/psum | solution.py:84
  314.8 1.9 fusion.40
  316.8 1.8 fusion.45
  318.6 61.8 %all-gather.2.cloned.1.call-done = bf16[1024,2432]{1,0:T(8,128)(2,1)} async-done(((bf16[64,2432]{1,0:T(8,128)(2,1)}), bf16[1024,2432]{1,0:T(8,128)(2,1)}) %all-gather.2.cloned.1.call-update) | async-done | bytes 4980752 | tf_op jit(solution)/shard_map/all_gather | solution.py:92
  380.4 4.5 convolution_convert_fusion
  385.0 1.8 fusion.41
  386.8 108.1 %all-reduce.2.cloned.1.call-done = bf16[192,2432]{1,0:T(8,128)(2,1)} async-done(((bf16[192,2432]{1,0:T(8,128)(2,1)}), bf16[192,2432]{1,0:T(8,128)(2,1)}) %all-reduce.2.cloned.1.call-update) | async-done | bytes 933904 | tf_op jit(solution)/shard_map/psum | solution.py:96
  494.9 2.5 convert_multiply_fusion
  (58 shorter events, 14.2 us)
Async XLA Ops:
  7.2 131.2 %copy-start = (bf16[192,2432]{1,0:T(8,128)(2,1)S(1)}, bf16[192,2432]{1,0:T(8,128)(2,1)}, u32[]{:S(2)}) copy-start(bf16[192,2432]{1,0:T(8,128)(2,1)} %param.12) | copy-start | bytes 2801668
  16.6 1.5 copy-start.1
  42.3 16.4 %copy-start.6 = (s32[16,3]{0,1:T(4,128)S(1)}, s32[16,3]{0,1:T(4,128)}, u32[]{:S(2)}) copy-start(s32[16,3]{0,1:T(4,128)} %param.11) | copy-start | bytes 580
  51.0 39.3 %all-to-all-start = ((bf16[16,64,3,384]{3,1,2,0:T(8,128)(2,1)}), bf16[16,64,3,384]{3,1,2,0:T(8,128)(2,1)S(1)}, u32[]{:S(2)}, u32[]{:S(2)}) async-start(bf16[16,64,3,384]{3,1,2,0:T(8,128)(2,1)} %reshape.134), calls=%async_computation | async-start | bytes 4718592 | tf_op jit(solution)/shard_map/all_to_all | solution.py:63
  58.6 221.5 %reduce-scatter.2.cloned.1.call-start = ((), (), s32[]{:S(2)}) async-start(), calls=%async_computation.2 | async-start | bytes 21168128 | tf_op jit(solution)/shard_map/reduce_scatter | solution.py:76
  98.4 1.0 copy-start.2
  98.4 1.0 copy-start.3
  98.5 1.1 copy-start.4
  113.5 1.0 copy-start.2
  113.5 1.0 copy-start.3
  113.5 1.1 copy-start.4
  128.5 1.0 copy-start.2
  128.5 1.0 copy-start.3
  128.6 1.1 copy-start.4
  146.7 168.1 %copy-start.5 = (bf16[1,64,2432]{2,1,0:T(8,128)(2,1)S(1)}, bf16[1,64,2432]{2,1,0:T(8,128)(2,1)}, u32[]{:S(2)}) copy-start(bf16[1,64,2432]{2,1,0:T(8,128)(2,1)} %param.13) | copy-start | bytes 933892
  146.7 233.7 %all-gather.2.cloned.1.call-start = ((), (), s32[]{:S(2)}) async-start(), calls=%async_computation.3 | async-start | bytes 5292032 | tf_op jit(solution)/shard_map/all_gather | solution.py:92
  316.7 178.2 %all-reduce.2.cloned.1.call-start = ((), (), s32[]{:S(2)}) async-start(), calls=%async_computation.4 | async-start | bytes 1867776 | tf_op jit(solution)/shard_map/psum | solution.py:96
Sparse Core Ops, SparseCore 0:
  146.8 133.2 reduce-scatter.1
  316.8 63.5 all-gather.1
  385.1 109.8 all-reduce.1
where the time goes:
time: 505 us; the launch traced here: 504 us
  waiting for transfers between devices  335 us (66%)
  local copies, waits for them, and re-layouts  60.8 us (12%)
  blocking collectives  32.1 us (6%)
  matrix products  28 us (6%)
  other arithmetic  25.8 us (5%)
  between operations  14.6 us (3%)
  starting transfers between devices  7.71 us (2%)
    reduce_scatter x1, waiting for transfers between devices, on_device(): lax.psum_scatter(jnp.einsum('rcj,jd->rcd', outputs_pair, out_weight, pref...  133 us
    psum x1, waiting for transfers between devices, on_device(): lax.psum(partial_grad.astype(jnp.bfloat16), 'dp').astype(jnp.float32)  108 us
    all_gather x1, waiting for transfers between devices, on_device(): lax.all_gather(upstream, 'tensor', axis=0, tiled=True)  61.8 us
    psum x1, blocking collectives, on_device(): squares = lax.psum(jnp.sum(tan_sum * tan_sum), 'tensor')  32.1 us
    all_to_all x1, waiting for transfers between devices, on_device(): lax.all_to_all(outgoing, 'tensor', split_axis=0, concat_axis=1, tiled=True)  31.4 us
    transpose x1, local copies, waits for them, and re-layouts, on_device(): outgoing.transpose(2, 0, 3, 1, 4)  12.2 us
  transfers between devices with their start and end apart: 4, of which 4 were waited for; matrix products, arithmetic and copies ran while one was open for 1% of the time, Pallas kernels for 0%

commit v1 on v0

v1 whole, which is shorter than its diff:
```python
import functools

import jax
import jax.numpy as jnp
from jax import lax
from jax.experimental import pallas as pl
from jax.experimental.pallas import tpu as pltpu
from jax.sharding import PartitionSpec as P

MESH = pl.DeviceIdType.MESH
F32 = jnp.float32
LOW = jnp.bfloat16


def swap_halves(value):
    return pltpu.roll(value, 64, 1)


def pack(n_t, slots, table, qkv, tan, outbox, live):
    low_half = lax.broadcasted_iota(jnp.int32, (1, 128), 1) < 64

    def one_device(t, carry):
        for s in range(slots):
            entry = table[t * slots + s]
            head = jnp.maximum(entry, 0)
            span = pl.ds(pl.multiple_of((head // 2) * 128, 128), 128)
            odd = jnp.full((1, 128), head % 2, jnp.int32) == 1
            live[s, t] = jnp.where(jnp.full((8, 128), entry, jnp.int32) >= 0, 1.0, 0.0)

            def pair(a, b, odd=odd):
                a = a.astype(F32)
                b = b.astype(F32)
                first = jnp.where(odd, swap_halves(a), a)
                second = jnp.where(odd, b, swap_halves(b))
                return jnp.where(low_half, first, second)

            outbox[s, t, :, 0:128] = (pair(tan[0, :, span], qkv[0, :, span]) * 0.125).astype(LOW)
            outbox[s, t, :, 128:256] = pair(qkv[1, :, span], tan[1, :, span]).astype(LOW)
            outbox[s, t, :, 256:384] = pair(qkv[2, :, span], tan[2, :, span]).astype(LOW)
        return carry

    lax.fori_loop(0, n_t, one_device, 0)


def body(
    dims,
    outbox,
    live,
    txt,
    weight,
    cot,
    image_out,
    tangent_out,
    grad_out,
    arrived,
    text_pad,
    score_rhs,
    value_rhs,
    attn,
    regroup,
    group_weight,
    proj_lhs,
    prim_t,
    part_out,
    part_in,
    tan_sum,
    squares,
    upstream,
    up_all,
    twin_out,
    twin_in,
    grad_send,
    grad_in,
    z_out,
    z_in,
    final,
    a_send,
    a_recv,
    w_send,
    w_recv,
    f_send,
    f_recv,
    own_sem,
    p_send,
    p_recv,
    r_send,
    r_recv,
    q_send,
    q_recv,
    u_send,
    u_recv,
    t_send,
    t_recv,
    g_send,
    g_recv,
    z_send,
    z_recv,
    c_send,
    c_recv,
    s_send,
    s_recv,
):
    n_t, side, n_z, slots, rows, keys, keys_pad, half, offset, width, txt_len = dims
    me = lax.axis_index("tensor")
    dp = lax.axis_index("dp")
    x = me // side
    y = me % side
    z = dp // 2
    c = dp % 2
    img = n_t * rows
    group_rows = side * rows

    def line(o, k):
        return (1 - o) * (x * side + k) + o * (k * side + y)

    def place(o):
        return (1 - o) * y + o * x

    def twin():
        return {"dp": z * 2 + (1 - c)}

    low_half = lax.broadcasted_iota(jnp.int32, (1, 128), 1) < 64

    for o in range(2):
        for k in range(side):
            group_weight[o, k * 256 + 192 : k * 256 + 256, :] = jnp.zeros((64, half), LOW)

    barrier = pltpu.get_barrier_semaphore()

    def greet(i, carry):
        t = ((x + i // side) % side) * side + (y + i % side) % side
        pl.semaphore_signal(barrier, inc=1, device_id={"tensor": t}, device_id_type=MESH)
        return carry

    lax.fori_loop(1, n_t, greet, 0)

    def greet_z(i, carry):
        pl.semaphore_signal(
            barrier, inc=1, device_id={"dp": ((z + i) % n_z) * 2 + c}, device_id_type=MESH
        )
        return carry

    lax.fori_loop(1, n_z, greet_z, 0)
    pl.semaphore_signal(barrier, inc=1, device_id=twin(), device_id_type=MESH)
    pl.semaphore_wait(barrier, n_t + n_z - 1)

    def in_copy(s, t):
        return pltpu.make_async_remote_copy(
            src_ref=outbox.at[s, t],
            dst_ref=arrived.at[s, me],
            send_sem=a_send.at[s, t],
            recv_sem=a_recv.at[s, me],
            device_id={"tensor": t},
            device_id_type=MESH,
        )

    def send_slot(s, carry):
        def send_one(i, inner):
            t = ((x + i // side) % side) * side + (y + i % side) % side
            in_copy(s, t).start()
            return inner

        lax.fori_loop(1, n_t, send_one, 0)
        pltpu.make_async_copy(outbox.at[s, me], arrived.at[s, me], own_sem.at[1 + s]).start()
        return carry

    lax.fori_loop(0, slots, send_slot, 0)

    half_at = pl.multiple_of(c * offset, 128)

    def w_copy(k):
        return pltpu.make_async_remote_copy(
            src_ref=weight.at[:, pl.ds(half_at, half)],
            dst_ref=group_weight.at[c, pl.ds(place(c) * 256, 192)],
            send_sem=w_send.at[k],
            recv_sem=w_recv.at[place(c)],
            device_id={"tensor": line(c, k)},
            device_id_type=MESH,
        )

    def w_own():
        return pltpu.make_async_copy(
            weight.at[:, pl.ds(half_at, half)],
            group_weight.at[c, pl.ds(place(c) * 256, 192)],
            own_sem.at[0],
        )

    def f_copy(k):
        return pltpu.make_async_remote_copy(
            src_ref=group_weight.at[c, pl.ds(k * 256, 192)],
            dst_ref=group_weight.at[c, pl.ds(k * 256, 192)],
            send_sem=f_send.at[k],
            recv_sem=f_recv.at[k],
            device_id=twin(),
            device_id_type=MESH,
        )

    def f_arrival(k):
        return pltpu.make_async_remote_copy(
            src_ref=group_weight.at[1 - c, pl.ds(k * 256, 192)],
            dst_ref=group_weight.at[1 - c, pl.ds(k * 256, 192)],
            send_sem=f_send.at[k],
            recv_sem=f_recv.at[k],
            device_id=twin(),
            device_id_type=MESH,
        )

    w_own().start()
    for i in range(1, side):
        w_copy((place(c) + i) % side).start()

    for s in range(slots):
        text_pad[320:384, :] = jnp.zeros((64, 256), LOW)
        text_pad[0:txt_len, :] = txt[s]
        kv = text_pad[:, 0:128].astype(F32)
        dkv = text_pad[:, 128:256].astype(F32)
        key_pair = jnp.where(low_half, kv, swap_halves(dkv))
        val_pair = jnp.where(low_half, swap_halves(kv), dkv)
        key_t = key_pair.T.astype(LOW)
        score_rhs[s, 0:64, 0:keys_pad] = jnp.zeros((64, keys_pad), LOW)
        score_rhs[s, 64:128, img:keys_pad] = key_t[0:64]
        score_rhs[s, :, keys_pad + img : 2 * keys_pad] = key_t
        value_rhs[s, img:keys_pad, :] = val_pair.astype(LOW)
        value_rhs[s, keys_pad + img : 2 * keys_pad, :] = jnp.where(low_half, 0.0, kv).astype(LOW)

    def p_copy(s, o, k):
        source = attn.at[s, :, k] if o == 0 else attn.at[s, k]
        return pltpu.make_async_remote_copy(
            src_ref=source,
            dst_ref=regroup.at[o, s, place(o)],
            send_sem=p_send.at[o, s, k],
            recv_sem=p_recv.at[o, s, place(o)],
            device_id={"tensor": line(o, k)},
            device_id_type=MESH,
        )

    def one_slot(s, carry):
        def arrival(i, inner):
            t = (me + i) % n_t
            pltpu.make_async_remote_copy(
                src_ref=outbox.at[s, t],
                dst_ref=arrived.at[s, t],
                send_sem=a_send.at[s, t],
                recv_sem=a_recv.at[s, t],
                device_id={"tensor": t},
                device_id_type=MESH,
            ).wait_recv()
            return inner

        lax.fori_loop(1, n_t, arrival, 0)
        pltpu.make_async_copy(outbox.at[s, me], arrived.at[s, me], own_sem.at[1 + s]).wait()
        key_t = arrived[s, :, :, 128:256].reshape(img, 128).astype(F32).T.astype(LOW)
        score_rhs[s, 64:128, 0:img] = key_t[0:64]
        score_rhs[s, :, keys_pad : keys_pad + img] = key_t
        val_pair = arrived[s, :, :, 256:384].reshape(img, 128)
        value_rhs[s, 0:img, :] = val_pair
        value_rhs[s, keys_pad : keys_pad + img, :] = jnp.where(
            low_half, 0.0, swap_halves(val_pair.astype(F32))
        ).astype(LOW)
        filled = live[s, me, 0:1, :]

        def one_block(q, inner):
            lhs = arrived[s, pl.ds(q * side, side), :, 0:128].reshape(group_rows, 128)
            scores = jnp.dot(lhs, score_rhs[s, :, 0:keys_pad], preferred_element_type=F32)
            tangents = jnp.dot(
                lhs, score_rhs[s, :, keys_pad : 2 * keys_pad], preferred_element_type=F32
            )
            valid = lax.broadcasted_iota(jnp.int32, (1, 128), 1) < keys - (keys_pad - 128)
            scores = jnp.concatenate(
                [
                    scores[:, : keys_pad - 128],
                    jnp.where(valid, scores[:, keys_pad - 128 :], -1e30),
                ],
                1,
            )
            top = jnp.max(scores, axis=1, keepdims=True)
            raised = jnp.exp(scores - top)
            total = jnp.sum(raised, axis=1, keepdims=True)
            mean = jnp.sum(raised * tangents, axis=1, keepdims=True) / total
            shifted = raised * (tangents - mean)
            joined = jnp.dot(
                raised.astype(LOW), value_rhs[s, 0:keys_pad, :], preferred_element_type=F32
            ) + jnp.dot(
                shifted.astype(LOW),
                value_rhs[s, keys_pad : 2 * keys_pad, :],
                preferred_element_type=F32,
            )
            joined = (joined / total * filled).astype(LOW)
            attn[s, q] = joined.reshape(side, rows, 128)
            return inner

        lax.fori_loop(0, side, one_block, 0)
        for o in range(2):
            own = place(o)
            for i in range(1, side):
                p_copy(s, o, (own + i) % side).start()
        regroup[0, s, y] = attn[s, :, y]
        regroup[1, s, x] = attn[s, x]

        @pl.when(s == slots - 2)
        def _():
            w_own().wait()
            for i in range(1, side):
                k = (place(c) + i) % side
                pltpu.make_async_remote_copy(
                    src_ref=weight.at[:, pl.ds(half_at, half)],
                    dst_ref=group_weight.at[c, pl.ds(k * 256, 192)],
                    send_sem=w_send.at[k],
                    recv_sem=w_recv.at[k],
                    device_id={"tensor": line(c, k)},
                    device_id_type=MESH,
                ).wait_recv()
            for k in range(side):
                f_copy(k).start()

        return carry

    lax.fori_loop(0, slots, one_slot, 0)

    def r_copy(o, j, k):
        span = pl.ds(pl.multiple_of(j * (half // 2), 128), half // 2)
        return pltpu.make_async_remote_copy(
            src_ref=part_out.at[o, k, :, :, span],
            dst_ref=part_in.at[o, place(1 - o), :, :, span],
            send_sem=r_send.at[o, j, k],
            recv_sem=r_recv.at[o, j, place(1 - o)],
            device_id={"tensor": line(1 - o, k)},
            device_id_type=MESH,
        )

    for k in range(side):
        f_arrival(k).wait_recv()

    for o in range(2):
        for s in range(slots):
            for i in range(1, side):
                k = (place(o) + i) % side
                pltpu.make_async_remote_copy(
                    src_ref=regroup.at[o, s, k],
                    dst_ref=regroup.at[o, s, k],
                    send_sem=p_send.at[o, s, k],
                    recv_sem=p_recv.at[o, s, k],
                    device_id={"tensor": line(o, k)},
                    device_id_type=MESH,
                ).wait_recv()

        def arrange(k, carry, o=o):
            first = regroup[o, 0, k].reshape(group_rows, 128).astype(F32)
            second = regroup[o, 1, k].reshape(group_rows, 128).astype(F32)
            third = regroup[o, 2, k].reshape(group_rows, 128).astype(F32)
            prim = jnp.where(low_half, first, swap_halves(second))
            prim_last = jnp.where(low_half, third, 0.0)
            tang = jnp.where(low_half, swap_halves(first), second)
            tang_last = jnp.where(low_half, swap_halves(third), 0.0)
            at = pl.multiple_of(k * 256, 256)
            proj_lhs[o, 0:group_rows, pl.ds(at, 128)] = prim.astype(LOW)
            proj_lhs[o, 0:group_rows, pl.ds(at + 128, 128)] = prim_last.astype(LOW)
            proj_lhs[o, group_rows : 2 * group_rows, pl.ds(at, 128)] = tang.astype(LOW)
            proj_lhs[o, group_rows : 2 * group_rows, pl.ds(at + 128, 128)] = tang_last.astype(LOW)
            prim_t[o, k, 0:128, :] = prim.T.astype(LOW)
            prim_t[o, k, 128:192, :] = prim_last.T[0:64].astype(LOW)
            return carry

        lax.fori_loop(0, side, arrange, 0)

        def project(j, carry, o=o):
            span = pl.ds(pl.multiple_of(j * (half // 2), 128), half // 2)
            part = jnp.dot(
                proj_lhs[o], group_weight[o, :, span], preferred_element_type=F32
            ).astype(LOW)
            for k in range(side):
                for kind in range(2):
                    at = kind * group_rows + k * rows
                    part_out[o, k, kind, :, span] = part[at : at + rows]
            own = place(1 - o)
            for i in range(1, side):
                r_copy(o, j, (own + i) % side).start()
            part_in[o, own, :, :, span] = part_out[o, own, :, :, span]
            return carry

        lax.fori_loop(0, 2, project, 0)

    for o in range(2):
        for j in range(2):
            for i in range(1, side):
                k = (place(1 - o) + i) % side
                span = pl.ds(j * (half // 2), half // 2)
                pltpu.make_async_remote_copy(
                    src_ref=part_out.at[o, k, :, :, span],
                    dst_ref=part_in.at[o, k, :, :, span],
                    send_sem=r_send.at[o, j, k],
                    recv_sem=r_recv.at[o, j, k],
                    device_id={"tensor": line(1 - o, k)},
                    device_id_type=MESH,
                ).wait_recv()

    def collect(o, kind, lo):
        total = part_in[o, 0, kind, :, lo:].astype(F32)
        for k in range(1, side):
            total = total + part_in[o, k, kind, :, lo:].astype(F32)
        return total

    skip = 2 * half - width
    tan_left = collect(0, 1, 0)
    tan_right = collect(1, 1, skip)
    tan_sum[:, 0:half] = tan_left
    tan_sum[:, half:width] = tan_right

    def sum_all(value):
        return jnp.sum(jnp.sum(value, axis=0, keepdims=True), axis=1, keepdims=True)

    own_squares = sum_all(tan_left * tan_left) + sum_all(tan_right * tan_right)
    squares[me] = jnp.broadcast_to(own_squares, (8, 128))

    def q_copy(t):
        return pltpu.make_async_remote_copy(
            src_ref=squares.at[me],
            dst_ref=squares.at[me],
            send_sem=q_send.at[t],
            recv_sem=q_recv.at[me],
            device_id={"tensor": t},
            device_id_type=MESH,
        )

    def q_start(i, carry):
        q_copy((me + i) % n_t).start()
        return carry

    lax.fori_loop(1, n_t, q_start, 0)
    image_out[:, 0:half] = collect(0, 0, 0).astype(LOW)
    image_out[:, half:width] = collect(1, 0, skip).astype(LOW)

    def q_wait(i, carry):
        t = (me + i) % n_t
        pltpu.make_async_remote_copy(
            src_ref=squares.at[t],
            dst_ref=squares.at[t],
            send_sem=q_send.at[t],
            recv_sem=q_recv.at[t],
            device_id={"tensor": t},
            device_id_type=MESH,
        ).wait_recv()
        return carry

    lax.fori_loop(1, n_t, q_wait, 0)
    square_sum = jnp.sum(squares[...], axis=0)[0:1, 0:1]
    divisor = jnp.sqrt(square_sum / (img * width)) + 0.1
    normal = (tan_sum[...] / divisor).astype(LOW)
    tangent_out[...] = normal
    upstream[...] = (cot[...].astype(F32) - normal.astype(F32)).astype(LOW)

    def u_copy(o, k):
        return pltpu.make_async_remote_copy(
            src_ref=upstream.at[:, pl.ds(o * offset, half)],
            dst_ref=up_all.at[o, pl.ds(place(1 - o) * rows, rows)],
            send_sem=u_send.at[o, k],
            recv_sem=u_recv.at[o, place(1 - o)],
            device_id={"tensor": line(1 - o, k)},
            device_id_type=MESH,
        )

    for o in range(2):
        own = place(1 - o)
        for i in range(1, side):
            u_copy(o, (own + i) % side).start()
        up_all[o, pl.ds(own * rows, rows), :] = upstream[:, o * offset : o * offset + half]

    for o in range(2):
        for i in range(1, side):
            k = (place(1 - o) + i) % side
            pltpu.make_async_remote_copy(
                src_ref=upstream.at[:, pl.ds(o * offset, half)],
                dst_ref=up_all.at[o, pl.ds(k * rows, rows)],
                send_sem=u_send.at[o, k],
                recv_sem=u_recv.at[o, k],
                device_id={"tensor": line(1 - o, k)},
                device_id_type=MESH,
            ).wait_recv()

    def t_copy(k):
        return pltpu.make_async_remote_copy(
            src_ref=twin_out.at[k],
            dst_ref=twin_in.at[k],
            send_sem=t_send.at[k],
            recv_sem=t_recv.at[k],
            device_id=twin(),
            device_id_type=MESH,
        )

    def g_copy(k):
        return pltpu.make_async_remote_copy(
            src_ref=grad_send.at[k],
            dst_ref=grad_in.at[place(c)],
            send_sem=g_send.at[k],
            recv_sem=g_recv.at[place(c)],
            device_id={"tensor": line(c, k)},
            device_id_type=MESH,
        )

    def for_twin(i, carry):
        k = (place(c) + i) % side
        twin_out[k] = jnp.dot(
            prim_t[1 - c, k], up_all[1 - c], preferred_element_type=F32
        ).astype(LOW)
        t_copy(k).start()
        return carry

    lax.fori_loop(1, side + 1, for_twin, 0)

    def for_line(i, carry):
        k = (place(c) + i) % side
        mine = jnp.dot(prim_t[c, k], up_all[c], preferred_element_type=F32)
        t_copy(k).wait_recv()
        grad_send[k] = (mine + twin_in[k].astype(F32)).astype(LOW)

        @pl.when(i < side)
        def _():
            g_copy(k).start()

        return carry

    lax.fori_loop(1, side + 1, for_line, 0)
    own = place(c)
    for i in range(1, side):
        k = (own + i) % side
        pltpu.make_async_remote_copy(
            src_ref=grad_send.at[k],
            dst_ref=grad_in.at[k],
            send_sem=g_send.at[k],
            recv_sem=g_recv.at[k],
            device_id={"tensor": line(c, k)},
            device_id_type=MESH,
        ).wait_recv()
    grad_in[own] = grad_send[own]
    total = grad_in[0].astype(F32)
    for k in range(1, side):
        total = total + grad_in[k].astype(F32)
    z_out[...] = total.astype(LOW)

    chunk_rows = 48
    chunk_cols = half // 2

    def chunk(k):
        return (
            pl.ds(pl.multiple_of((k // 2) * chunk_rows, 16), chunk_rows),
            pl.ds(pl.multiple_of((k % 2) * chunk_cols, 128), chunk_cols),
        )

    def z_copy(k, source):
        return pltpu.make_async_remote_copy(
            src_ref=z_out.at[chunk(k)],
            dst_ref=z_in.at[source],
            send_sem=z_send.at[k],
            recv_sem=z_recv.at[source],
            device_id={"dp": k * 2 + c},
            device_id_type=MESH,
        )

    def c_copy(k, owner):
        return pltpu.make_async_remote_copy(
            src_ref=final.at[(c,) + chunk(owner)],
            dst_ref=final.at[(c,) + chunk(owner)],
            send_sem=c_send.at[k],
            recv_sem=c_recv.at[owner],
            device_id={"dp": k * 2 + c},
            device_id_type=MESH,
        )

    def z_loop(step):
        def one(i, carry):
            step((z + i) % n_z)
            return carry

        lax.fori_loop(1, n_z, one, 0)

    z_loop(lambda k: z_copy(k, z).start())
    z_in[z] = z_out[chunk(z)]
    z_loop(lambda k: z_copy(k, k).wait_recv())
    total = z_in[0].astype(F32)
    for k in range(1, n_z):
        total = total + z_in[k].astype(F32)
    final[(c,) + chunk(z)] = (total * (1.0 / (2 * n_z))).astype(LOW)
    z_loop(lambda k: c_copy(k, z).start())
    z_loop(lambda k: c_copy(k, k).wait_recv())

    def s_copy(which):
        return pltpu.make_async_remote_copy(
            src_ref=final.at[which],
            dst_ref=final.at[which],
            send_sem=s_send,
            recv_sem=s_recv,
            device_id=twin(),
            device_id_type=MESH,
        )

    s_copy(c).start()

    def sent_in(s, carry):
        def one(i, inner):
            in_copy(s, (me + i) % n_t).wait_send()
            return inner

        lax.fori_loop(1, n_t, one, 0)
        return carry

    lax.fori_loop(0, slots, sent_in, 0)
    for i in range(1, side):
        w_copy((place(c) + i) % side).wait_send()
        g_copy((place(c) + i) % side).wait_send()
        for o in range(2):
            for s in range(slots):
                p_copy(s, o, (place(o) + i) % side).wait_send()
            for j in range(2):
                r_copy(o, j, (place(1 - o) + i) % side).wait_send()
            u_copy(o, (place(1 - o) + i) % side).wait_send()
    for k in range(side):
        f_copy(k).wait_send()
        t_copy(k).wait_send()

    def q_sent(i, carry):
        q_copy((me + i) % n_t).wait_send()
        return carry

    lax.fori_loop(1, n_t, q_sent, 0)
    z_loop(lambda k: z_copy(k, z).wait_send())
    z_loop(lambda k: c_copy(k, z).wait_send())
    s_copy(c).wait_send()
    s_copy(1 - c).wait_recv()
    grad_out[:, 0:half] = final[0].astype(F32)
    grad_out[:, half:width] = final[1, :, skip:].astype(F32)


def on_device(n_t, n_dp, qkv_img, tan_img, txt_kv, head_table, out_weight, cotangent):
    rows, width = qkv_img.shape[1], qkv_img.shape[3]
    slots = head_table.shape[1]
    side = 4
    n_z = n_dp // 2
    txt_len = txt_kv.shape[2]
    img = n_t * rows
    keys = img + txt_len
    keys_pad = -(-keys // 128) * 128
    half = -(-width // 256) * 128
    offset = width - half
    dims = (n_t, side, n_z, slots, rows, keys, keys_pad, half, offset, width, txt_len)
    dma = pltpu.SemaphoreType.DMA
    vmem = pl.BlockSpec(memory_space=pltpu.VMEM)
    lines = (2, side)
    outbox, live = pl.pallas_call(
        functools.partial(pack, n_t, slots),
        out_shape=(
            jax.ShapeDtypeStruct((slots, n_t, rows, 384), LOW),
            jax.ShapeDtypeStruct((slots, n_t, 8, 128), F32),
        ),
        in_specs=[pl.BlockSpec(memory_space=pltpu.SMEM), vmem, vmem],
        out_specs=(vmem, vmem),
    )(
        head_table.reshape(-1),
        jnp.transpose(qkv_img[0], (1, 0, 2)),
        jnp.transpose(tan_img[0], (1, 0, 2)),
    )
    return pl.pallas_call(
        functools.partial(body, dims),
        out_shape=(
            jax.ShapeDtypeStruct((rows, width), LOW),
            jax.ShapeDtypeStruct((rows, width), LOW),
            jax.ShapeDtypeStruct((slots * 64, width), F32),
        ),
        in_specs=[pl.BlockSpec(memory_space=pl.ANY)] + [vmem] * 4,
        out_specs=(vmem, vmem, vmem),
        scratch_shapes=[
            pltpu.VMEM((slots, n_t, rows, 384), LOW),
            pltpu.VMEM((384, 256), LOW),
            pltpu.VMEM((slots, 128, 2 * keys_pad), LOW),
            pltpu.VMEM((slots, 2 * keys_pad, 128), LOW),
            pltpu.VMEM((slots, side, side, rows, 128), LOW),
            pltpu.VMEM((2, slots, side, side, rows, 128), LOW),
            pltpu.VMEM((2, side * 256, half), LOW),
            pltpu.VMEM((2, 2 * side * rows, side * 256), LOW),
            pltpu.VMEM((2, side, 192, side * rows), LOW),
            pltpu.VMEM((2, side, 2, rows, half), LOW),
            pltpu.VMEM((2, side, 2, rows, half), LOW),
            pltpu.VMEM((rows, width), F32),
            pltpu.VMEM((n_t, 8, 128), F32),
            pltpu.VMEM((rows, width), LOW),
            pltpu.VMEM((2, side * rows, half), LOW),
            pltpu.VMEM((side, 192, half), LOW),
            pltpu.VMEM((side, 192, half), LOW),
            pltpu.VMEM((side, 192, half), LOW),
            pltpu.VMEM((side, 192, half), LOW),
            pltpu.VMEM((192, half), LOW),
            pltpu.VMEM((n_z, 48, half // 2), LOW),
            pltpu.VMEM((2, 192, half), LOW),
            dma((slots, n_t)),
            dma((slots, n_t)),
            dma((side,)),
            dma((side,)),
            dma((side,)),
            dma((side,)),
            dma((1 + slots,)),
            dma((2, slots, side)),
            dma((2, slots, side)),
            dma((2, 2, side)),
            dma((2, 2, side)),
            dma((n_t,)),
            dma((n_t,)),
            dma(lines),
            dma(lines),
            dma((side,)),
            dma((side,)),
            dma((side,)),
            dma((side,)),
            dma((n_z,)),
            dma((n_z,)),
            dma((n_z,)),
            dma((n_z,)),
            dma,
            dma,
        ],
        compiler_params=pltpu.CompilerParams(
            collective_id=0, has_side_effects=True, vmem_limit_bytes=56 * 1024 * 1024
        ),
    )(
        outbox,
        live,
        txt_kv[0],
        out_weight,
        cotangent[0],
    )


def solution(mesh):
    n_t, n_dp = mesh.shape["tensor"], mesh.shape["dp"]

    def step(*args):
        image_out, tangent_out, weight_grad = on_device(n_t, n_dp, *args)
        return image_out[None], tangent_out[None], weight_grad

    return jax.shard_map(
        step,
        mesh=mesh,
        in_specs=(
            P("dp", "tensor", None, None),
            P("dp", "tensor", None, None),
            P("dp", "tensor", None, None),
            P(),
            P("tensor", None),
            P("dp", "tensor", None),
        ),
        out_specs=(P("dp", "tensor", None), P("dp", "tensor", None), P("tensor", None)),
        check_vma=False,
    )
```

time: 505 us -> 162 us (0.32)
  waiting for transfers between devices: 335 us -> 0 us
  Pallas kernels: 0 us -> 154 us
  local copies, waits for them, and re-layouts: 60.8 us -> 7.64 us
  blocking collectives: 32.1 us -> 0 us
  matrix products: 28 us -> 0 us
  other arithmetic: 25.8 us -> 0 us
  between operations: 14.6 us -> 0.64 us
  starting transfers between devices: 7.71 us -> 0 us
    pallas_call x0 -> x2, Pallas kernels: none -> 154 us  [the longest x1 148 us: on_device(): pl.pallas_call(functools.partial(body, dims), out_shape=(jax.ShapeDtypeSt...]
    reduce_scatter x1 -> x0, waiting for transfers between devices: 133 us -> none  [on_device(): lax.psum_scatter(jnp.einsum('rcj,jd->rcd', outputs_pair, out_weight, pref...]
    psum x1 -> x0, waiting for transfers between devices: 108 us -> none  [on_device(): lax.psum(partial_grad.astype(jnp.bfloat16), 'dp').astype(jnp.float32)]
    all_gather x1 -> x0, waiting for transfers between devices: 61.8 us -> none  [on_device(): lax.all_gather(upstream, 'tensor', axis=0, tiled=True)]
    psum x1 -> x0, blocking collectives: 32.1 us -> none  [on_device(): squares = lax.psum(jnp.sum(tan_sum * tan_sum), 'tensor')]
    all_to_all x1 -> x0, waiting for transfers between devices: 31.4 us -> none  [on_device(): lax.all_to_all(outgoing, 'tensor', split_axis=0, concat_axis=1, tiled=True)]
    dot_general x14 -> x0, matrix products: 28 us -> none  [the longest x1 8.31 us: on_device(): jnp.einsum('rcj,jd->rcd', outputs_pair, out_weight, preferred_element_typ...]
    concatenate x7 -> x0, local copies, waits for them, and re-layouts: 12.3 us -> none  [the longest x4 8.14 us: on_device(): jnp.concatenate([qkv_img[0], tan_img[0]], 1)]
  transfers between devices with their start and end apart: 4 -> 0, of which waited for: 4 -> 0; matrix products, arithmetic and copies ran while one was open for 1% -> 0% of each run, Pallas kernels for 0% -> 0%
where the time goes in v1:
time: 162 us
  Pallas kernels  154 us (95%)
  local copies, waits for them, and re-layouts  7.64 us (5%)
    pallas_call x1, Pallas kernels, on_device(): pl.pallas_call(functools.partial(body, dims), out_shape=(jax.ShapeDtypeSt...  148 us
    unnamed x4, local copies, waits for them, and re-layouts  7.04 us
    pallas_call x1, Pallas kernels, on_device(): pl.pallas_call(functools.partial(pack, n_t, slots), out_shape=(jax.ShapeD...  5.47 us

profile of v1, /device:TPU:1, one launch (start us, length us, event | category | flops | bytes accessed | tf_op | source)
XLA Modules:
  0.0 162.1 jit_solution(12142148384361930186)
XLA Ops:
  0.6 0.8 copy.10
  1.4 0.6 reshape.9.table
  2.0 5.5 %shard_map.85 = (bf16[3,16,64,384]{3,2,1,0:T(8,128)(2,1)}, f32[3,16,8,128]{3,2,1,0:T(8,128)}) custom-call(s32[48]{0:T(128)} %reshape.9.table, bf16[3,64,2432]{2,1,0:T(8,128)(2,1)} %bitcast.10, bf16[3,64,2432]{2,1,0:T(8,128)(2,1)} %bitcast.11), custom_call_target="tpu_custom_call" | custom-call | tf_op jit(solution)/shard_map/pallas_call | solution.py:648
  7.5 148.3 %shard_map.86 = (bf16[64,2432]{1,0:T(8,128)(2,1)}, bf16[64,2432]{1,0:T(8,128)(2,1)}, f32[192,2432]{1,0:T(8,128)}) custom-call(bf16[3,16,64,384]{3,2,1,0:T(8,128)(2,1)} %get-tuple-element.8.outbox, f32[3,16,8,128]{3,2,1,0:T(8,128)} %get-tuple-element.9.live, bf16[3,333,256]{2,1,0:T(8,128)(2,1)} %bitcast.12, bf16[192,2432]{1,0:T(8,128)(2,1)} %weight.1, ...), custom_call_target="tpu_custom_call" | custom-call | tf_op jit(solution)/shard_map/pallas_call | solution.py:661
  155.8 1.7 %copy.14 = bf16[1,64,2432]{2,1,0:T(8,128)(2,1)} copy(bf16[1,64,2432]{2,1,0:T(8,128)(2,1)} %bitcast.15) | data formatting | bytes 622592
  157.5 1.7 %copy.15 = bf16[1,64,2432]{2,1,0:T(8,128)(2,1)} copy(bf16[1,64,2432]{2,1,0:T(8,128)(2,1)} %bitcast.14) | data formatting | bytes 622592
  159.2 2.9 %copy.16 = f32[192,2432]{1,0:T(8,128)} copy(f32[192,2432]{1,0:T(8,128)} %get-tuple-element.18) | data formatting | bytes 3735552

commit v2 on v1

v2 whole, which is shorter than its diff:
```python
import functools

import jax
import jax.numpy as jnp
from jax import lax
from jax.experimental import pallas as pl
from jax.experimental.pallas import tpu as pltpu
from jax.sharding import PartitionSpec as P

MESH = pl.DeviceIdType.MESH
F32 = jnp.float32
LOW = jnp.bfloat16


def swap_halves(value):
    return pltpu.roll(value, 64, 1)


def finish(image, tangent, grad, image_out, tangent_out, grad_out):
    half = 2 * grad.shape[3]
    part = grad.shape[3]
    width = image.shape[1]
    image_out[...] = image[...]
    tangent_out[...] = tangent[...]
    grad_out[:, 0:part] = grad[0, 0].astype(F32)
    grad_out[:, part:half] = grad[0, 1].astype(F32)
    skip = 2 * half - width
    grad_out[:, half : half + part - skip] = grad[1, 0, :, skip:].astype(F32)
    grad_out[:, half + part - skip : width] = grad[1, 1].astype(F32)


def body(
    dims,
    table,
    qkv,
    tan,
    txt,
    weight,
    cot,
    image_out,
    tangent_out,
    grad_out,
    cot_local,
    staged,
    outbox,
    arrived,
    text_pad,
    score_rhs,
    value_rhs,
    attn,
    regroup,
    group_weight,
    proj_lhs,
    prim_t,
    part_out,
    part_in,
    tan_sum,
    squares,
    upstream,
    up_all,
    twin_out,
    twin_in,
    grad_send,
    grad_in,
    z_out,
    z_in,
    final,
    a_send,
    a_recv,
    w_send,
    w_recv,
    x_send,
    x_recv,
    f_send,
    f_recv,
    own_sem,
    p_send,
    p_recv,
    r_send,
    r_recv,
    q_send,
    q_recv,
    u_send,
    u_recv,
    t_send,
    t_recv,
    g_send,
    g_recv,
    z_send,
    z_recv,
    c_send,
    c_recv,
    s_send,
    s_recv,
):
    n_t, side, n_z, slots, rows, keys, keys_pad, half, offset, width, txt_len = dims
    me = lax.axis_index("tensor")
    dp = lax.axis_index("dp")
    x = me // side
    y = me % side
    z = dp // 2
    c = dp % 2
    img = n_t * rows
    group_rows = side * rows

    def line(o, k):
        return (1 - o) * (x * side + k) + o * (k * side + y)

    def place(o):
        return (1 - o) * y + o * x

    def twin():
        return {"dp": z * 2 + (1 - c)}

    low_half = lax.broadcasted_iota(jnp.int32, (1, 128), 1) < 64

    barrier = pltpu.get_barrier_semaphore()

    def greet(i, carry):
        t = ((x + i // side) % side) * side + (y + i % side) % side
        pl.semaphore_signal(barrier, inc=1, device_id={"tensor": t}, device_id_type=MESH)
        return carry

    lax.fori_loop(1, n_t, greet, 0)

    def greet_z(i, carry):
        pl.semaphore_signal(
            barrier, inc=1, device_id={"dp": ((z + i) % n_z) * 2 + c}, device_id_type=MESH
        )
        return carry

    lax.fori_loop(1, n_z, greet_z, 0)
    pl.semaphore_signal(barrier, inc=1, device_id=twin(), device_id_type=MESH)
    cot_copy = pltpu.make_async_copy(cot, cot_local, own_sem.at[1 + slots])
    cot_copy.start()

    for o in range(2):
        for k in range(side):
            group_weight[o, k * 256 + 192 : k * 256 + 256, :] = jnp.zeros((64, half), LOW)

    def text_rows(s):
        text_pad[320:384, :] = jnp.zeros((64, 256), LOW)
        text_pad[0:txt_len, :] = txt[s]
        kv = text_pad[:, 0:128].astype(F32)
        dkv = text_pad[:, 128:256].astype(F32)
        key_pair = jnp.where(low_half, kv, swap_halves(dkv))
        val_pair = jnp.where(low_half, swap_halves(kv), dkv)
        key_t = key_pair.T.astype(LOW)
        score_rhs[s, 0:64, 0:keys_pad] = jnp.zeros((64, keys_pad), LOW)
        score_rhs[s, 64:128, img:keys_pad] = key_t[0:64]
        score_rhs[s, :, keys_pad + img : 2 * keys_pad] = key_t
        value_rhs[s, img:keys_pad, :] = val_pair.astype(LOW)
        value_rhs[s, keys_pad + img : 2 * keys_pad, :] = jnp.where(low_half, 0.0, kv).astype(LOW)

    for kind in range(3):
        for page in range(width // 128):
            staged[kind, page] = qkv[kind, :, page * 128 : page * 128 + 128]
            staged[3 + kind, page] = tan[kind, :, page * 128 : page * 128 + 128]

    def pick(s, t):
        head = jnp.maximum(table[s, t], 0)
        page = lax.shift_right_logical(head, 1)
        odd = jnp.full((1, 128), lax.bitwise_and(head, 1), jnp.int32) == 1

        def pair(first, second):
            a = staged[first, page]
            b = staged[second, page]
            return jnp.where(
                low_half, jnp.where(odd, swap_halves(a), a), jnp.where(odd, b, swap_halves(b))
            )

        outbox[s, t, :, 0:128] = pair(3, 0) * jnp.asarray(0.125, LOW)
        outbox[s, t, :, 128:256] = pair(1, 4)
        outbox[s, t, :, 256:384] = pair(2, 5)

    pl.semaphore_wait(barrier, n_t + n_z - 1)

    def in_copy(s, t):
        return pltpu.make_async_remote_copy(
            src_ref=outbox.at[s, t],
            dst_ref=arrived.at[s, me],
            send_sem=a_send.at[s, t],
            recv_sem=a_recv.at[s, me],
            device_id={"tensor": t},
            device_id_type=MESH,
        )

    def ring(step):
        def one(i, carry):
            step(((x + i // side) % side) * side + (y + i % side) % side)
            return carry

        lax.fori_loop(1, n_t, one, 0)

    def in_own(s):
        return pltpu.make_async_copy(outbox.at[s, me], arrived.at[s, me], own_sem.at[1 + s])

    half_at = pl.multiple_of(c * offset, 128)

    chunk_rows = 2 * 192 // n_z
    chunk_cols = half // 2

    def w_span(k, at):
        return (
            pl.ds(pl.multiple_of(k * 256 + (at // 2) * chunk_rows, 16), chunk_rows),
            pl.ds(pl.multiple_of((at % 2) * chunk_cols, 128), chunk_cols),
        )

    def w_copy(k):
        return pltpu.make_async_remote_copy(
            src_ref=weight.at[
                pl.ds(pl.multiple_of((z // 2) * chunk_rows, 16), chunk_rows),
                pl.ds(pl.multiple_of(c * offset + (z % 2) * chunk_cols, 128), chunk_cols),
            ],
            dst_ref=group_weight.at[(c,) + w_span(place(c), z)],
            send_sem=w_send.at[k],
            recv_sem=w_recv.at[place(c)],
            device_id={"tensor": line(c, k)},
            device_id_type=MESH,
        )

    def w_arrival(k):
        return pltpu.make_async_remote_copy(
            src_ref=group_weight.at[(c,) + w_span(k, z)],
            dst_ref=group_weight.at[(c,) + w_span(k, z)],
            send_sem=w_send.at[k],
            recv_sem=w_recv.at[k],
            device_id={"tensor": line(c, k)},
            device_id_type=MESH,
        )

    def x_copy(k, at, other):
        return pltpu.make_async_remote_copy(
            src_ref=group_weight.at[(c,) + w_span(k, at)],
            dst_ref=group_weight.at[(c,) + w_span(k, at)],
            send_sem=x_send.at[k, other],
            recv_sem=x_recv.at[k, at],
            device_id={"dp": other * 2 + c},
            device_id_type=MESH,
        )

    def x_loop(step):
        def one(i, carry):
            for n in range(1, side):
                step((place(c) + n) % side, (z + i) % n_z)
            return carry

        lax.fori_loop(1, n_z, one, 0)

    def w_own():
        return pltpu.make_async_copy(
            weight.at[:, pl.ds(half_at, half)],
            group_weight.at[c, pl.ds(place(c) * 256, 192)],
            own_sem.at[0],
        )

    def f_copy(k):
        return pltpu.make_async_remote_copy(
            src_ref=group_weight.at[c, pl.ds(k * 256, 192)],
            dst_ref=group_weight.at[c, pl.ds(k * 256, 192)],
            send_sem=f_send.at[k],
            recv_sem=f_recv.at[k],
            device_id=twin(),
            device_id_type=MESH,
        )

    def f_arrival(k):
        return pltpu.make_async_remote_copy(
            src_ref=group_weight.at[1 - c, pl.ds(k * 256, 192)],
            dst_ref=group_weight.at[1 - c, pl.ds(k * 256, 192)],
            send_sem=f_send.at[k],
            recv_sem=f_recv.at[k],
            device_id=twin(),
            device_id_type=MESH,
        )

    w_own().start()
    for i in range(1, side):
        w_copy((place(c) + i) % side).start()

    def depart(s):
        def one(t):
            pick(s, t)
            in_copy(s, t).start()

        ring(one)

    depart(0)
    depart(1)
    ring(lambda t: pick(2, t))
    for s in range(slots):
        pick(s, me)
        in_own(s).start()
        text_rows(s)

    for i in range(1, side):
        w_arrival((place(c) + i) % side).wait_recv()
    x_loop(lambda k, other: x_copy(k, z, other).start())

    def p_copy(s, o, k):
        source = attn.at[s, :, k] if o == 0 else attn.at[s, k]
        return pltpu.make_async_remote_copy(
            src_ref=source,
            dst_ref=regroup.at[o, s, place(o)],
            send_sem=p_send.at[o, s, k],
            recv_sem=p_recv.at[o, s, place(o)],
            device_id={"tensor": line(o, k)},
            device_id_type=MESH,
        )

    def one_slot(s, carry):
        @pl.when(s == 0)
        def _():
            def step(t):
                in_copy(0, t).wait_send()
                in_copy(2, t).start()

            ring(step)

        def arrival(i, inner):
            t = (me + i) % n_t
            pltpu.make_async_remote_copy(
                src_ref=outbox.at[s, t],
                dst_ref=arrived.at[s, t],
                send_sem=a_send.at[s, t],
                recv_sem=a_recv.at[s, t],
                device_id={"tensor": t},
                device_id_type=MESH,
            ).wait_recv()
            return inner

        lax.fori_loop(1, n_t, arrival, 0)
        in_own(s).wait()
        key_t = arrived[s, :, :, 128:256].reshape(img, 128).astype(F32).T.astype(LOW)
        score_rhs[s, 64:128, 0:img] = key_t[0:64]
        score_rhs[s, :, keys_pad : keys_pad + img] = key_t
        val_pair = arrived[s, :, :, 256:384].reshape(img, 128)
        value_rhs[s, 0:img, :] = val_pair
        value_rhs[s, keys_pad : keys_pad + img, :] = jnp.where(
            low_half, 0.0, swap_halves(val_pair.astype(F32))
        ).astype(LOW)
        filled = jnp.where(jnp.full((1, 128), table[s, me], jnp.int32) >= 0, 1.0, 0.0)

        def one_block(q, inner):
            lhs = arrived[s, pl.ds(q * side, side), :, 0:128].reshape(group_rows, 128)
            scores = jnp.dot(lhs, score_rhs[s, :, 0:keys_pad], preferred_element_type=F32)
            tangents = jnp.dot(
                lhs, score_rhs[s, :, keys_pad : 2 * keys_pad], preferred_element_type=F32
            )
            valid = lax.broadcasted_iota(jnp.int32, (1, 128), 1) < keys - (keys_pad - 128)
            scores = jnp.concatenate(
                [
                    scores[:, : keys_pad - 128],
                    jnp.where(valid, scores[:, keys_pad - 128 :], -1e30),
                ],
                1,
            )
            top = jnp.max(scores, axis=1, keepdims=True)
            raised = jnp.exp(scores - top)
            total = jnp.sum(raised, axis=1, keepdims=True)
            mean = jnp.sum(raised * tangents, axis=1, keepdims=True) / total
            shifted = raised * (tangents - mean)
            joined = jnp.dot(
                raised.astype(LOW), value_rhs[s, 0:keys_pad, :], preferred_element_type=F32
            ) + jnp.dot(
                shifted.astype(LOW),
                value_rhs[s, keys_pad : 2 * keys_pad, :],
                preferred_element_type=F32,
            )
            joined = (joined / total * filled).astype(LOW)
            attn[s, q] = joined.reshape(side, rows, 128)
            return inner

        lax.fori_loop(0, side, one_block, 0)
        for o in range(2):
            own = place(o)
            for i in range(1, side):
                p_copy(s, o, (own + i) % side).start()
        regroup[0, s, y] = attn[s, :, y]
        regroup[1, s, x] = attn[s, x]

        return carry

    lax.fori_loop(0, slots, one_slot, 0)

    w_own().wait()
    x_loop(lambda k, other: x_copy(k, other, other).wait_recv())
    for k in range(side):
        f_copy(k).start()

    def r_copy(kind, o, j, k):
        span = pl.ds(pl.multiple_of(j * 256, 256), 256)
        return pltpu.make_async_remote_copy(
            src_ref=part_out.at[kind, o, k, :, span],
            dst_ref=part_in.at[kind, o, place(1 - o), :, span],
            send_sem=r_send.at[kind, o, j, k],
            recv_sem=r_recv.at[kind, o, j, place(1 - o)],
            device_id={"tensor": line(1 - o, k)},
            device_id_type=MESH,
        )

    def r_arrival(kind, o, j, k):
        span = pl.ds(pl.multiple_of(j * 256, 256), 256)
        return pltpu.make_async_remote_copy(
            src_ref=part_out.at[kind, o, k, :, span],
            dst_ref=part_in.at[kind, o, k, :, span],
            send_sem=r_send.at[kind, o, j, k],
            recv_sem=r_recv.at[kind, o, j, k],
            device_id={"tensor": line(1 - o, k)},
            device_id_type=MESH,
        )

    for o in range(2):
        for s in range(slots):
            for i in range(1, side):
                k = (place(o) + i) % side
                pltpu.make_async_remote_copy(
                    src_ref=regroup.at[o, s, k],
                    dst_ref=regroup.at[o, s, k],
                    send_sem=p_send.at[o, s, k],
                    recv_sem=p_recv.at[o, s, k],
                    device_id={"tensor": line(o, k)},
                    device_id_type=MESH,
                ).wait_recv()

        def tangents_of(k, carry, o=o):
            first = regroup[o, 0, k].reshape(group_rows, 128).astype(F32)
            second = regroup[o, 1, k].reshape(group_rows, 128).astype(F32)
            third = regroup[o, 2, k].reshape(group_rows, 128).astype(F32)
            tang = jnp.where(low_half, swap_halves(first), second)
            tang_last = jnp.where(low_half, swap_halves(third), 0.0)
            at = pl.multiple_of(k * 256, 256)
            proj_lhs[1, o, :, pl.ds(at, 128)] = tang.astype(LOW)
            proj_lhs[1, o, :, pl.ds(at + 128, 128)] = tang_last.astype(LOW)
            return carry

        lax.fori_loop(0, side, tangents_of, 0)

    for k in range(side):
        f_arrival(k).wait_recv()

    steps = half // 256

    def project(kind):
        def one(n, carry):
            o = n % 2
            j = n // 2
            span = pl.ds(pl.multiple_of(j * 256, 256), 256)
            part = jnp.dot(
                proj_lhs[kind, o], group_weight[o, :, span], preferred_element_type=F32
            ).astype(LOW)
            for k in range(side):
                part_out[kind, o, k, :, span] = part[k * rows : (k + 1) * rows]
            own = place(1 - o)
            for i in range(1, side):
                r_copy(kind, o, j, (own + i) % side).start()
            part_in[kind, o, own, :, span] = part_out[kind, o, own, :, span]
            return carry

        lax.fori_loop(0, 2 * steps, one, 0)

    def gathered(kind):
        def one(n, carry):
            for i in range(1, side):
                r_arrival(kind, n % 2, n // 2, (place(1 - n % 2) + i) % side).wait_recv()
            return carry

        lax.fori_loop(0, 2 * steps, one, 0)

    project(1)

    for o in range(2):

        def prims_of(k, carry, o=o):
            first = regroup[o, 0, k].reshape(group_rows, 128).astype(F32)
            second = regroup[o, 1, k].reshape(group_rows, 128).astype(F32)
            third = regroup[o, 2, k].reshape(group_rows, 128).astype(F32)
            prim = jnp.where(low_half, first, swap_halves(second))
            prim_last = jnp.where(low_half, third, 0.0)
            at = pl.multiple_of(k * 256, 256)
            proj_lhs[0, o, :, pl.ds(at, 128)] = prim.astype(LOW)
            proj_lhs[0, o, :, pl.ds(at + 128, 128)] = prim_last.astype(LOW)
            prim_t[o, k, 0:128, :] = prim.T.astype(LOW)
            prim_t[o, k, 128:192, :] = prim_last.T[0:64].astype(LOW)
            return carry

        lax.fori_loop(0, side, prims_of, 0)

    gathered(1)

    def collect(o, kind, lo):
        total = part_in[kind, o, 0, :, lo:].astype(F32)
        for k in range(1, side):
            total = total + part_in[kind, o, k, :, lo:].astype(F32)
        return total

    skip = 2 * half - width
    tan_left = collect(0, 1, 0)
    tan_right = collect(1, 1, skip)
    tan_sum[:, 0:half] = tan_left
    tan_sum[:, half:width] = tan_right

    def sum_all(value):
        return jnp.sum(jnp.sum(value, axis=0, keepdims=True), axis=1, keepdims=True)

    own_squares = sum_all(tan_left * tan_left) + sum_all(tan_right * tan_right)
    squares[me] = jnp.broadcast_to(own_squares, (8, 128))

    def q_copy(t):
        return pltpu.make_async_remote_copy(
            src_ref=squares.at[me],
            dst_ref=squares.at[me],
            send_sem=q_send.at[t],
            recv_sem=q_recv.at[me],
            device_id={"tensor": t},
            device_id_type=MESH,
        )

    def q_start(i, carry):
        q_copy((me + i) % n_t).start()
        return carry

    lax.fori_loop(1, n_t, q_start, 0)
    def q_wait(i, carry):
        t = (me + i) % n_t
        pltpu.make_async_remote_copy(
            src_ref=squares.at[t],
            dst_ref=squares.at[t],
            send_sem=q_send.at[t],
            recv_sem=q_recv.at[t],
            device_id={"tensor": t},
            device_id_type=MESH,
        ).wait_recv()
        return carry

    lax.fori_loop(1, n_t, q_wait, 0)
    square_sum = jnp.sum(squares[...], axis=0)[0:1, 0:1]
    divisor = jnp.sqrt(square_sum / (img * width)) + 0.1
    normal = (tan_sum[...] / divisor).astype(LOW)
    tangent_out[...] = normal
    cot_copy.wait()
    upstream[...] = (cot_local[...].astype(F32) - normal.astype(F32)).astype(LOW)

    part = half // 2

    def u_copy(o, j, k):
        return pltpu.make_async_remote_copy(
            src_ref=upstream.at[:, pl.ds(o * offset + j * part, part)],
            dst_ref=up_all.at[o, j, pl.ds(place(1 - o) * rows, rows)],
            send_sem=u_send.at[o, j, k],
            recv_sem=u_recv.at[o, j, place(1 - o)],
            device_id={"tensor": line(1 - o, k)},
            device_id_type=MESH,
        )

    for j in range(2):
        for i in range(1, side):
            for o in range(2):
                u_copy(o, j, (place(1 - o) + i) % side).start()
    for j in range(2):
        for o in range(2):
            at = o * offset + j * part
            up_all[o, j, pl.ds(place(1 - o) * rows, rows), :] = upstream[:, at : at + part]

    def t_copy(j, k):
        return pltpu.make_async_remote_copy(
            src_ref=twin_out.at[j, k],
            dst_ref=twin_in.at[j, k],
            send_sem=t_send.at[j, k],
            recv_sem=t_recv.at[j, k],
            device_id=twin(),
            device_id_type=MESH,
        )

    def g_copy(j, k):
        return pltpu.make_async_remote_copy(
            src_ref=grad_send.at[j, k],
            dst_ref=grad_in.at[j, place(c)],
            send_sem=g_send.at[j, k],
            recv_sem=g_recv.at[j, place(c)],
            device_id={"tensor": line(c, k)},
            device_id_type=MESH,
        )

    own = place(c)

    def grad_part(j, carry):
        for o in range(2):
            for i in range(1, side):
                k = (place(1 - o) + i) % side
                pltpu.make_async_remote_copy(
                    src_ref=upstream.at[:, pl.ds(o * offset, part)],
                    dst_ref=up_all.at[o, j, pl.ds(k * rows, rows)],
                    send_sem=u_send.at[o, j, k],
                    recv_sem=u_recv.at[o, j, k],
                    device_id={"tensor": line(1 - o, k)},
                    device_id_type=MESH,
                ).wait_recv()

        def for_twin(i, inner):
            k = (own + i) % side
            twin_out[j, k] = jnp.dot(
                prim_t[1 - c, k], up_all[1 - c, j], preferred_element_type=F32
            ).astype(LOW)
            t_copy(j, k).start()
            return inner

        lax.fori_loop(1, side + 1, for_twin, 0)

        def for_line(i, inner):
            k = (own + i) % side
            mine = jnp.dot(prim_t[c, k], up_all[c, j], preferred_element_type=F32)
            t_copy(j, k).wait_recv()
            grad_send[j, k] = (mine + twin_in[j, k].astype(F32)).astype(LOW)

            @pl.when(i < side)
            def _():
                g_copy(j, k).start()

            return inner

        lax.fori_loop(1, side + 1, for_line, 0)
        grad_in[j, own] = grad_send[j, own]
        return carry

    lax.fori_loop(0, 2, grad_part, 0)

    def chunk(k):
        return (k % 2, pl.ds(pl.multiple_of((k // 2) * chunk_rows, 16), chunk_rows))

    def z_copy(k, source):
        return pltpu.make_async_remote_copy(
            src_ref=z_out.at[chunk(k)],
            dst_ref=z_in.at[source],
            send_sem=z_send.at[k],
            recv_sem=z_recv.at[source],
            device_id={"dp": k * 2 + c},
            device_id_type=MESH,
        )

    def c_copy(k, owner):
        return pltpu.make_async_remote_copy(
            src_ref=final.at[(c,) + chunk(owner)],
            dst_ref=final.at[(c,) + chunk(owner)],
            send_sem=c_send.at[k],
            recv_sem=c_recv.at[owner],
            device_id={"dp": k * 2 + c},
            device_id_type=MESH,
        )

    def z_loop(step):
        def one(i, carry):
            step((z + i) % n_z)
            return carry

        lax.fori_loop(1, n_z, one, 0)

    def to_owners(j, carry):
        for i in range(1, side):
            k = (own + i) % side
            pltpu.make_async_remote_copy(
                src_ref=grad_send.at[j, k],
                dst_ref=grad_in.at[j, k],
                send_sem=g_send.at[j, k],
                recv_sem=g_recv.at[j, k],
                device_id={"tensor": line(c, k)},
                device_id_type=MESH,
            ).wait_recv()
        total = grad_in[j, 0].astype(F32)
        for k in range(1, side):
            total = total + grad_in[j, k].astype(F32)
        z_out[j] = total.astype(LOW)

        def one(i, inner):
            k = (z + i) % n_z

            @pl.when(k % 2 == j)
            def _():
                z_copy(k, z).start()

            return inner

        lax.fori_loop(1, n_z, one, 0)
        return carry

    lax.fori_loop(0, 2, to_owners, 0)

    project(0)

    z_in[z] = z_out[chunk(z)]
    z_loop(lambda k: z_copy(k, k).wait_recv())
    total = z_in[0].astype(F32)
    for k in range(1, n_z):
        total = total + z_in[k].astype(F32)
    final[(c,) + chunk(z)] = (total * (1.0 / (2 * n_z))).astype(LOW)
    z_loop(lambda k: c_copy(k, z).start())
    gathered(0)
    image_out[:, 0:half] = collect(0, 0, 0).astype(LOW)
    image_out[:, half:width] = collect(1, 0, skip).astype(LOW)
    z_loop(lambda k: c_copy(k, k).wait_recv())

    def s_copy(which):
        return pltpu.make_async_remote_copy(
            src_ref=final.at[which],
            dst_ref=final.at[which],
            send_sem=s_send,
            recv_sem=s_recv,
            device_id=twin(),
            device_id_type=MESH,
        )

    s_copy(c).start()

    ring(lambda t: in_copy(1, t).wait_send())
    ring(lambda t: in_copy(2, t).wait_send())
    x_loop(lambda k, other: x_copy(k, z, other).wait_send())
    for i in range(1, side):
        w_copy((place(c) + i) % side).wait_send()
        for o in range(2):
            for s in range(slots):
                p_copy(s, o, (place(o) + i) % side).wait_send()
            for j in range(2):
                u_copy(o, j, (place(1 - o) + i) % side).wait_send()
        for j in range(2):
            g_copy(j, (place(c) + i) % side).wait_send()

    def r_sent(n, carry):
        o = n % 2
        for kind in range(2):
            for i in range(1, side):
                r_copy(kind, o, n // 2, (place(1 - o) + i) % side).wait_send()
        return carry

    lax.fori_loop(0, 2 * steps, r_sent, 0)
    for k in range(side):
        f_copy(k).wait_send()
        for j in range(2):
            t_copy(j, k).wait_send()

    def q_sent(i, carry):
        q_copy((me + i) % n_t).wait_send()
        return carry

    lax.fori_loop(1, n_t, q_sent, 0)
    z_loop(lambda k: z_copy(k, z).wait_send())
    z_loop(lambda k: c_copy(k, z).wait_send())
    s_copy(c).wait_send()
    s_copy(1 - c).wait_recv()
    grad_out[...] = final[...]


def on_device(n_t, n_dp, qkv_img, tan_img, txt_kv, head_table, out_weight, cotangent):
    rows, width = qkv_img.shape[1], qkv_img.shape[3]
    slots = head_table.shape[1]
    side = 4
    n_z = n_dp // 2
    txt_len = txt_kv.shape[2]
    img = n_t * rows
    keys = img + txt_len
    keys_pad = -(-keys // 128) * 128
    half = -(-width // 256) * 128
    offset = width - half
    dims = (n_t, side, n_z, slots, rows, keys, keys_pad, half, offset, width, txt_len)
    dma = pltpu.SemaphoreType.DMA
    vmem = pl.BlockSpec(memory_space=pltpu.VMEM)
    hbm = pl.BlockSpec(memory_space=pl.ANY)
    steps = half // 256
    image, tangent, grad = pl.pallas_call(
        functools.partial(body, dims),
        out_shape=(
            jax.ShapeDtypeStruct((rows, width), LOW),
            jax.ShapeDtypeStruct((rows, width), LOW),
            jax.ShapeDtypeStruct((2, 2, 192, half // 2), LOW),
        ),
        in_specs=[pl.BlockSpec(memory_space=pltpu.SMEM), vmem, vmem, vmem, hbm, hbm],
        out_specs=(vmem, vmem, vmem),
        scratch_shapes=[
            pltpu.VMEM((rows, width), LOW),
            pltpu.VMEM((6, width // 128, rows, 128), LOW),
            pltpu.VMEM((slots, n_t, rows, 384), LOW),
            pltpu.VMEM((slots, n_t, rows, 384), LOW),
            pltpu.VMEM((384, 256), LOW),
            pltpu.VMEM((slots, 128, 2 * keys_pad), LOW),
            pltpu.VMEM((slots, 2 * keys_pad, 128), LOW),
            pltpu.VMEM((slots, side, side, rows, 128), LOW),
            pltpu.VMEM((2, slots, side, side, rows, 128), LOW),
            pltpu.VMEM((2, side * 256, half), LOW),
            pltpu.VMEM((2, 2, side * rows, side * 256), LOW),
            pltpu.VMEM((2, side, 192, side * rows), LOW),
            pltpu.VMEM((2, 2, side, rows, half), LOW),
            pltpu.VMEM((2, 2, side, rows, half), LOW),
            pltpu.VMEM((rows, width), F32),
            pltpu.VMEM((n_t, 8, 128), F32),
            pltpu.VMEM((rows, width), LOW),
            pltpu.VMEM((2, 2, side * rows, half // 2), LOW),
            pltpu.VMEM((2, side, 192, half // 2), LOW),
            pltpu.VMEM((2, side, 192, half // 2), LOW),
            pltpu.VMEM((2, side, 192, half // 2), LOW),
            pltpu.VMEM((2, side, 192, half // 2), LOW),
            pltpu.VMEM((2, 192, half // 2), LOW),
            pltpu.VMEM((n_z, 2 * 192 // n_z, half // 2), LOW),
            pltpu.VMEM((2, 2, 192, half // 2), LOW),
            dma((slots, n_t)),
            dma((slots, n_t)),
            dma((side,)),
            dma((side,)),
            dma((side, n_z)),
            dma((side, n_z)),
            dma((side,)),
            dma((side,)),
            dma((2 + slots,)),
            dma((2, slots, side)),
            dma((2, slots, side)),
            dma((2, 2, steps, side)),
            dma((2, 2, steps, side)),
            dma((n_t,)),
            dma((n_t,)),
            dma((2, 2, side)),
            dma((2, 2, side)),
            dma((2, side)),
            dma((2, side)),
            dma((2, side)),
            dma((2, side)),
            dma((n_z,)),
            dma((n_z,)),
            dma((n_z,)),
            dma((n_z,)),
            dma,
            dma,
        ],
        compiler_params=pltpu.CompilerParams(
            collective_id=0, has_side_effects=True, vmem_limit_bytes=56 * 1024 * 1024
        ),
    )(
        head_table.T,
        jnp.transpose(qkv_img[0], (1, 0, 2)),
        jnp.transpose(tan_img[0], (1, 0, 2)),
        txt_kv[0],
        out_weight,
        cotangent[0],
    )
    parts = 4
    by_rows = pl.BlockSpec((rows // parts, width), lambda i: (i, 0))
    return pl.pallas_call(
        finish,
        grid=(parts,),
        out_shape=(
            jax.ShapeDtypeStruct((rows, width), LOW),
            jax.ShapeDtypeStruct((rows, width), LOW),
            jax.ShapeDtypeStruct((slots * 64, width), F32),
        ),
        in_specs=[
            by_rows,
            by_rows,
            pl.BlockSpec((2, 2, 192 // parts, half // 2), lambda i: (0, 0, i, 0)),
        ],
        out_specs=(by_rows, by_rows, pl.BlockSpec((192 // parts, width), lambda i: (i, 0))),
    )(image, tangent, grad)


def solution(mesh):
    n_t, n_dp = mesh.shape["tensor"], mesh.shape["dp"]

    def step(*args):
        image_out, tangent_out, weight_grad = on_device(n_t, n_dp, *args)
        return image_out[None], tangent_out[None], weight_grad

    return jax.shard_map(
        step,
        mesh=mesh,
        in_specs=(
            P("dp", "tensor", None, None),
            P("dp", "tensor", None, None),
            P("dp", "tensor", None, None),
            P(),
            P("tensor", None),
            P("dp", "tensor", None),
        ),
        out_specs=(P("dp", "tensor", None), P("dp", "tensor", None), P("tensor", None)),
        check_vma=False,
    )
```

time: 162 us -> 132 us (0.81)
  Pallas kernels: 154 us -> 131 us
  local copies, waits for them, and re-layouts: 7.64 us -> 0 us
    pallas_call x1, Pallas kernels: 148 us -> 127 us  [on_device(): pl.pallas_call(functools.partial(body, dims), out_shape=(jax.ShapeDtypeSt...]
    unnamed x4 -> x0, local copies, waits for them, and re-layouts: 7.04 us -> none
    pallas_call x1, Pallas kernels: 5.47 us -> 3.8 us  [on_device(): pl.pallas_call(finish, grid=(parts,), out_shape=(jax.ShapeDtypeStruct((ro...]
where the time goes in v2:
time: 132 us; the launch traced here: 131 us
  Pallas kernels  131 us (99%)
    pallas_call x1, Pallas kernels, on_device(): pl.pallas_call(functools.partial(body, dims), out_shape=(jax.ShapeDtypeSt...  127 us
    pallas_call x1, Pallas kernels, on_device(): pl.pallas_call(finish, grid=(parts,), out_shape=(jax.ShapeDtypeStruct((ro...  3.8 us

profile of v2, /device:TPU:1, one launch (start us, length us, event | category | flops | bytes accessed | tf_op | source)
XLA Modules:
  0.0 131.3 jit_solution(12581073209638668092)
XLA Ops:
  0.6 126.9 %shard_map.85 = (bf16[64,2432]{1,0:T(8,128)(2,1)}, bf16[64,2432]{1,0:T(8,128)(2,1)}, bf16[2,2,192,640]{3,2,1,0:T(8,128)(2,1)}) custom-call(s32[3,16]{1,0:T(4,128)} %bitcast.15, bf16[3,64,2432]{2,1,0:T(8,128)(2,1)} %bitcast.11, bf16[3,64,2432]{2,1,0:T(8,128)(2,1)} %bitcast.12, bf16[3,333,256]{2,1,0:T(8,128)(2,1)} %bitcast.13, bf16[192,2432]{1,0:T(8,128)(2,1)} %weight.1, ...), custom_call_target="tpu_custom_call" | custom-call | tf_op jit(solution)/shard_map/pallas_call | solution.py:768
  127.5 3.8 %shard_map.86 = (bf16[64,2432]{1,0:T(8,128)(2,1)}, bf16[64,2432]{1,0:T(8,128)(2,1)}, f32[192,2432]{1,0:T(8,128)}) custom-call(bf16[64,2432]{1,0:T(8,128)(2,1)} %get-tuple-element.9.image, bf16[64,2432]{1,0:T(8,128)(2,1)} %get-tuple-element.10.tangent, bf16[2,2,192,640]{3,2,1,0:T(8,128)(2,1)} %get-tuple-element.11.grad), custom_call_target="tpu_custom_call" | custom-call | tf_op jit(solution)/shard_map/pallas_call | solution.py:844

commit v3 on v2

--- a/solution.py
+++ b/solution.py
@@ -16,17 +16,48 @@
     return pltpu.roll(value, 64, 1)
 
 
-def finish(image, tangent, grad, image_out, tangent_out, grad_out):
-    half = 2 * grad.shape[3]
-    part = grad.shape[3]
+def finish(
+    image, tangent, grad, image_out, tangent_out, grad_out, pair, held, wide, in_sem, out_sem, way_sem
+):
+    half = grad.shape[2]
     width = image.shape[1]
-    image_out[...] = image[...]
-    tangent_out[...] = tangent[...]
-    grad_out[:, 0:part] = grad[0, 0].astype(F32)
-    grad_out[:, part:half] = grad[0, 1].astype(F32)
     skip = 2 * half - width
-    grad_out[:, half : half + part - skip] = grad[1, 0, :, skip:].astype(F32)
-    grad_out[:, half + part - skip : width] = grad[1, 1].astype(F32)
+    blocks = 4
+    tall = grad.shape[1] // blocks
+
+    def load(i):
+        rows = pl.ds(i * tall, tall)
+        return pltpu.make_async_copy(grad.at[:, rows], held.at[:, rows], in_sem.at[i])
+
+    def store(i):
+        rows = pl.ds(i * tall, tall)
+        return pltpu.make_async_copy(wide.at[rows], grad_out.at[rows], out_sem.at[i])
+
+    for i in range(blocks):
+        load(i).start()
+    there = (
+        pltpu.make_async_copy(image, pair.at[0], way_sem.at[0]),
+        pltpu.make_async_copy(tangent, pair.at[1], way_sem.at[1]),
+    )
+    back = (
+        pltpu.make_async_copy(pair.at[0], image_out, way_sem.at[2]),
+        pltpu.make_async_copy(pair.at[1], tangent_out, way_sem.at[3]),
+    )
+    for copy in there:
+        copy.start()
+    for i in range(blocks):
+        load(i).wait()
+        rows = pl.ds(i * tall, tall)
+        wide[rows, 0:half] = held[0, rows].astype(F32)
+        wide[rows, half:width] = held[1, rows, skip:].astype(F32)
+        store(i).start()
+    for copy, after in zip(there, back):
+        copy.wait()
+        after.start()
+    for i in range(blocks):
+        store(i).wait()
+    for copy in back:
+        copy.wait()
 
 
 def body(
@@ -41,6 +72,9 @@
     tangent_out,
     grad_out,
     cot_local,
+    qkv_local,
+    tan_local,
+    txt_local,
     staged,
     outbox,
     arrived,
@@ -114,6 +148,18 @@
 
     low_half = lax.broadcasted_iota(jnp.int32, (1, 128), 1) < 64
 
+    cot_copy = pltpu.make_async_copy(cot, cot_local, own_sem.at[1 + slots])
+    txt_copy = pltpu.make_async_copy(txt, txt_local, own_sem.at[2 + slots])
+    loads = [
+        pltpu.make_async_copy(whole.at[kind], local.at[kind], own_sem.at[3 + slots + 3 * n + kind])
+        for n, (whole, local) in enumerate(((qkv, qkv_local), (tan, tan_local)))
+        for kind in range(3)
+    ]
+    for copy in loads:
+        copy.start()
+    txt_copy.start()
+    cot_copy.start()
+
     barrier = pltpu.get_barrier_semaphore()
 
     def greet(i, carry):
@@ -131,8 +177,6 @@
 
     lax.fori_loop(1, n_z, greet_z, 0)
     pl.semaphore_signal(barrier, inc=1, device_id=twin(), device_id_type=MESH)
-    cot_copy = pltpu.make_async_copy(cot, cot_local, own_sem.at[1 + slots])
-    cot_copy.start()
 
     for o in range(2):
         for k in range(side):
@@ -140,7 +184,7 @@
 
     def text_rows(s):
         text_pad[320:384, :] = jnp.zeros((64, 256), LOW)
-        text_pad[0:txt_len, :] = txt[s]
+        text_pad[0:txt_len, :] = txt_local[s]
         kv = text_pad[:, 0:128].astype(F32)
         dkv = text_pad[:, 128:256].astype(F32)
         key_pair = jnp.where(low_half, kv, swap_halves(dkv))
@@ -152,10 +196,11 @@
         value_rhs[s, img:keys_pad, :] = val_pair.astype(LOW)
         value_rhs[s, keys_pad + img : 2 * keys_pad, :] = jnp.where(low_half, 0.0, kv).astype(LOW)
 
-    for kind in range(3):
-        for page in range(width // 128):
-            staged[kind, page] = qkv[kind, :, page * 128 : page * 128 + 128]
-            staged[3 + kind, page] = tan[kind, :, page * 128 : page * 128 + 128]
+    for n, local in enumerate((qkv_local, tan_local)):
+        for kind in range(3):
+            loads[3 * n + kind].wait()
+            for page in range(width // 128):
+                staged[3 * n + kind, page] = local[kind, :, page * 128 : page * 128 + 128]
 
     def pick(s, t):
         head = jnp.maximum(table[s, t], 0)
@@ -229,23 +274,37 @@
             device_id_type=MESH,
         )
 
-    def x_copy(k, at, other):
+    def x_copy(k, at, way, hop):
         return pltpu.make_async_remote_copy(
             src_ref=group_weight.at[(c,) + w_span(k, at)],
             dst_ref=group_weight.at[(c,) + w_span(k, at)],
-            send_sem=x_send.at[k, other],
+            send_sem=x_send.at[k, way, hop],
             recv_sem=x_recv.at[k, at],
-            device_id={"dp": other * 2 + c},
-            device_id_type=MESH,
-        )
-
-    def x_loop(step):
-        def one(i, carry):
-            for n in range(1, side):
-                step((place(c) + n) % side, (z + i) % n_z)
-            return carry
-
-        lax.fori_loop(1, n_z, one, 0)
+            device_id={"dp": ((z + 1 - 2 * way + n_z) % n_z) * 2 + c},
+            device_id_type=MESH,
+        )
+
+    reach = (n_z // 2, n_z // 2 - 1)
+
+    def x_step(hop):
+        for way in range(2):
+            if hop >= 1 and hop <= reach[way]:
+                at = (z + (2 * way - 1) * hop + n_z) % n_z
+                for i in range(1, side):
+                    k = (place(c) + i) % side
+                    x_copy(k, at, way, hop % side).wait_recv()
+                    if hop < reach[way]:
+                        x_copy(k, at, way, hop).start()
+            if hop == 0:
+                for i in range(1, side):
+                    x_copy((place(c) + i) % side, z, way, 0).start()
+
+    def x_sent():
+        for way in range(2):
+            for hop in range(reach[way]):
+                at = (z + (2 * way - 1) * hop + n_z) % n_z
+                for i in range(1, side):
+                    x_copy((place(c) + i) % side, at, way, hop).wait_send()
 
     def w_own():
         return pltpu.make_async_copy(
@@ -285,38 +344,53 @@
 
         ring(one)
 
-    depart(0)
+    ring(lambda t: pick(0, t))
+    for i in range(1, side):
+        w_arrival((place(c) + i) % side).wait_recv()
+    x_step(0)
+    ring(lambda t: in_copy(0, t).start())
     depart(1)
-    ring(lambda t: pick(2, t))
+    txt_copy.wait()
     for s in range(slots):
         pick(s, me)
         in_own(s).start()
         text_rows(s)
-
-    for i in range(1, side):
-        w_arrival((place(c) + i) % side).wait_recv()
-    x_loop(lambda k, other: x_copy(k, z, other).start())
-
-    def p_copy(s, o, k):
-        source = attn.at[s, :, k] if o == 0 else attn.at[s, k]
+    x_step(1)
+    ring(lambda t: pick(2, t))
+    x_step(2)
+
+    def last_slot(t):
+        in_copy(0, t).wait_send()
+        in_copy(2, t).start()
+
+    ring(last_slot)
+
+    def p_copy(s, o, k, q):
+        if o == 0:
+            source, target = attn.at[s, q, k], regroup.at[0, s, y, q]
+        else:
+            source, target = attn.at[s, k], regroup.at[1, s, x]
         return pltpu.make_async_remote_copy(
             src_ref=source,
-            dst_ref=regroup.at[o, s, place(o)],
-            send_sem=p_send.at[o, s, k],
-            recv_sem=p_recv.at[o, s, place(o)],
+            dst_ref=target,
+            send_sem=p_send.at[o, s, k, q],
+            recv_sem=p_recv.at[o, s, place(o), q],
             device_id={"tensor": line(o, k)},
             device_id_type=MESH,
         )
 
+    def p_arrival(s, o, k, q):
+        target = regroup.at[0, s, k, q] if o == 0 else regroup.at[1, s, k]
+        return pltpu.make_async_remote_copy(
+            src_ref=target,
+            dst_ref=target,
+            send_sem=p_send.at[o, s, k, q],
+            recv_sem=p_recv.at[o, s, k, q],
+            device_id={"tensor": line(o, k)},
+            device_id_type=MESH,
+        )
+
     def one_slot(s, carry):
-        @pl.when(s == 0)
-        def _():
-            def step(t):
-                in_copy(0, t).wait_send()
-                in_copy(2, t).start()
-
-            ring(step)
-
         def arrival(i, inner):
             t = (me + i) % n_t
             pltpu.make_async_remote_copy(
@@ -341,7 +415,8 @@
         ).astype(LOW)
         filled = jnp.where(jnp.full((1, 128), table[s, me], jnp.int32) >= 0, 1.0, 0.0)
 
-        def one_block(q, inner):
+        def one_block(turn, inner):
+            q = (x + 1 + turn) % side
             lhs = arrived[s, pl.ds(q * side, side), :, 0:128].reshape(group_rows, 128)
             scores = jnp.dot(lhs, score_rhs[s, :, 0:keys_pad], preferred_element_type=F32)
             tangents = jnp.dot(
@@ -369,24 +444,34 @@
             )
             joined = (joined / total * filled).astype(LOW)
             attn[s, q] = joined.reshape(side, rows, 128)
+            for i in range(1, side):
+                p_copy(s, 0, (y + i) % side, q).start()
+
+            @pl.when(turn < side - 1)
+            def _():
+                p_copy(s, 1, q, 0).start()
+
             return inner
 
         lax.fori_loop(0, side, one_block, 0)
-        for o in range(2):
-            own = place(o)
-            for i in range(1, side):
-                p_copy(s, o, (own + i) % side).start()
         regroup[0, s, y] = attn[s, :, y]
         regroup[1, s, x] = attn[s, x]
 
+        @pl.when(s == 0)
+        def _():
+            x_step(3)
+
+        @pl.when(s == 1)
+        def _():
+            x_step(4)
+            w_own().wait()
+            for k in range(side):
+                f_copy(k).start()
+
+
         return carry
 
     lax.fori_loop(0, slots, one_slot, 0)
-
-    w_own().wait()
-    x_loop(lambda k, other: x_copy(k, other, other).wait_recv())
-    for k in range(side):
-        f_copy(k).start()
 
     def r_copy(kind, o, j, k):
         span = pl.ds(pl.multiple_of(j * 256, 256), 256)
@@ -414,14 +499,8 @@
         for s in range(slots):
             for i in range(1, side):
                 k = (place(o) + i) % side
-                pltpu.make_async_remote_copy(
-                    src_ref=regroup.at[o, s, k],
-                    dst_ref=regroup.at[o, s, k],
-                    send_sem=p_send.at[o, s, k],
-                    recv_sem=p_recv.at[o, s, k],
-                    device_id={"tensor": line(o, k)},
-                    device_id_type=MESH,
-                ).wait_recv()
+                for q in range(side if o == 0 else 1):
+                    p_arrival(s, o, k, q).wait_recv()
 
         def tangents_of(k, carry, o=o):
             first = regroup[o, 0, k].reshape(group_rows, 128).astype(F32)
@@ -486,25 +565,27 @@
 
         lax.fori_loop(0, side, prims_of, 0)
 
-    gathered(1)
-
-    def collect(o, kind, lo):
-        total = part_in[kind, o, 0, :, lo:].astype(F32)
+    skip = 2 * half - width
+
+    def collect(kind, o, first, last):
+        total = part_in[kind, o, 0, :, first:last].astype(F32)
         for k in range(1, side):
-            total = total + part_in[kind, o, k, :, lo:].astype(F32)
+            total = total + part_in[kind, o, k, :, first:last].astype(F32)
         return total
 
-    skip = 2 * half - width
-    tan_left = collect(0, 1, 0)
-    tan_right = collect(1, 1, skip)
-    tan_sum[:, 0:half] = tan_left
-    tan_sum[:, half:width] = tan_right
-
-    def sum_all(value):
-        return jnp.sum(jnp.sum(value, axis=0, keepdims=True), axis=1, keepdims=True)
-
-    own_squares = sum_all(tan_left * tan_left) + sum_all(tan_right * tan_right)
-    squares[me] = jnp.broadcast_to(own_squares, (8, 128))
+    own_squares = jnp.zeros((1, 128), F32)
+    for n in range(2 * steps):
+        o, j = n % 2, n // 2
+        for i in range(1, side):
+            r_arrival(1, o, j, (place(1 - o) + i) % side).wait_recv()
+        first = max(j * 256, skip * o)
+        columns = collect(1, o, first, j * 256 + 256)
+        at = o * offset + first
+        tan_sum[:, at : at + columns.shape[1]] = columns
+        column_squares = jnp.sum(columns * columns, axis=0, keepdims=True)
+        for lane in range(0, columns.shape[1], 128):
+            own_squares = own_squares + column_squares[:, lane : lane + 128]
+    squares[me] = jnp.broadcast_to(jnp.sum(own_squares, axis=1, keepdims=True), (8, 128))
 
     def q_copy(t):
         return pltpu.make_async_remote_copy(
@@ -541,99 +622,124 @@
     cot_copy.wait()
     upstream[...] = (cot_local[...].astype(F32) - normal.astype(F32)).astype(LOW)
 
-    part = half // 2
-
-    def u_copy(o, j, k):
-        return pltpu.make_async_remote_copy(
-            src_ref=upstream.at[:, pl.ds(o * offset + j * part, part)],
-            dst_ref=up_all.at[o, j, pl.ds(place(1 - o) * rows, rows)],
-            send_sem=u_send.at[o, j, k],
-            recv_sem=u_recv.at[o, j, place(1 - o)],
+    starts = (0, 384, 640, 1024)
+    sizes = (384, 256, 384, 256)
+
+    def cut(p):
+        return pl.ds(starts[p], sizes[p])
+
+    def u_copy(o, p, k):
+        return pltpu.make_async_remote_copy(
+            src_ref=upstream.at[:, pl.ds(o * offset + starts[p], sizes[p])],
+            dst_ref=up_all.at[o, pl.ds(place(1 - o) * rows, rows), cut(p)],
+            send_sem=u_send.at[o, p, k],
+            recv_sem=u_recv.at[o, p, place(1 - o)],
             device_id={"tensor": line(1 - o, k)},
             device_id_type=MESH,
         )
 
-    for j in range(2):
+    def u_arrival(o, p, k):
+        return pltpu.make_async_remote_copy(
+            src_ref=up_all.at[o, pl.ds(k * rows, rows), cut(p)],
+            dst_ref=up_all.at[o, pl.ds(k * rows, rows), cut(p)],
+            send_sem=u_send.at[o, p, k],
+            recv_sem=u_recv.at[o, p, k],
+            device_id={"tensor": line(1 - o, k)},
+            device_id_type=MESH,
+        )
+
+    def up_leaves(p):
         for i in range(1, side):
             for o in range(2):
-                u_copy(o, j, (place(1 - o) + i) % side).start()
-    for j in range(2):
-        for o in range(2):
-            at = o * offset + j * part
-            up_all[o, j, pl.ds(place(1 - o) * rows, rows), :] = upstream[:, at : at + part]
-
-    def t_copy(j, k):
-        return pltpu.make_async_remote_copy(
-            src_ref=twin_out.at[j, k],
-            dst_ref=twin_in.at[j, k],
-            send_sem=t_send.at[j, k],
-            recv_sem=t_recv.at[j, k],
+                k = (place(1 - o) + i) % side
+                if p > 0:
+                    u_copy(o, p - 1, k).wait_send()
+                u_copy(o, p, k).start()
+
+    up_leaves(0)
+    for o in range(2):
+        up_all[o, pl.ds(place(1 - o) * rows, rows), :] = upstream[:, o * offset : o * offset + half]
+    up_leaves(1)
+
+    def t_copy(p, k):
+        return pltpu.make_async_remote_copy(
+            src_ref=twin_out.at[k, :, cut(p)],
+            dst_ref=twin_in.at[k, :, cut(p)],
+            send_sem=t_send.at[p, k],
+            recv_sem=t_recv.at[p, k],
             device_id=twin(),
             device_id_type=MESH,
         )
 
-    def g_copy(j, k):
-        return pltpu.make_async_remote_copy(
-            src_ref=grad_send.at[j, k],
-            dst_ref=grad_in.at[j, place(c)],
-            send_sem=g_send.at[j, k],
-            recv_sem=g_recv.at[j, place(c)],
+    def g_copy(p, k):
+        return pltpu.make_async_remote_copy(
+            src_ref=grad_send.at[k, :, cut(p)],
+            dst_ref=grad_in.at[place(c), :, cut(p)],
+            send_sem=g_send.at[p, k],
+            recv_sem=g_recv.at[p, place(c)],
             device_id={"tensor": line(c, k)},
             device_id_type=MESH,
         )
 
+    def g_arrival(p, k):
+        return pltpu.make_async_remote_copy(
+            src_ref=grad_in.at[k, :, cut(p)],
+            dst_ref=grad_in.at[k, :, cut(p)],
+            send_sem=g_send.at[p, k],
+            recv_sem=g_recv.at[p, k],
+            device_id={"tensor": line(c, k)},
+            device_id_type=MESH,
+        )
+
     own = place(c)
 
-    def grad_part(j, carry):
+    def grad_part(p):
         for o in range(2):
             for i in range(1, side):
-                k = (place(1 - o) + i) % side
-                pltpu.make_async_remote_copy(
-                    src_ref=upstream.at[:, pl.ds(o * offset, part)],
-                    dst_ref=up_all.at[o, j, pl.ds(k * rows, rows)],
-                    send_sem=u_send.at[o, j, k],
-                    recv_sem=u_recv.at[o, j, k],
-                    device_id={"tensor": line(1 - o, k)},
-                    device_id_type=MESH,
-                ).wait_recv()
+                u_arrival(o, p, (place(1 - o) + i) % side).wait_recv()
+        if p + 2 < 4:
+            up_leaves(p + 2)
 
         def for_twin(i, inner):
             k = (own + i) % side
-            twin_out[j, k] = jnp.dot(
-                prim_t[1 - c, k], up_all[1 - c, j], preferred_element_type=F32
+            twin_out[k, :, cut(p)] = jnp.dot(
+                prim_t[1 - c, k], up_all[1 - c, :, cut(p)], preferred_element_type=F32
             ).astype(LOW)
-            t_copy(j, k).start()
+            t_copy(p, k).start()
             return inner
 
         lax.fori_loop(1, side + 1, for_twin, 0)
 
         def for_line(i, inner):
             k = (own + i) % side
-            mine = jnp.dot(prim_t[c, k], up_all[c, j], preferred_element_type=F32)
-            t_copy(j, k).wait_recv()
-            grad_send[j, k] = (mine + twin_in[j, k].astype(F32)).astype(LOW)
+            mine = jnp.dot(prim_t[c, k], up_all[c, :, cut(p)], preferred_element_type=F32)
+            t_copy(p, k).wait_recv()
+            grad_send[k, :, cut(p)] = (mine + twin_in[k, :, cut(p)].astype(F32)).astype(LOW)
 
             @pl.when(i < side)
             def _():
-                g_copy(j, k).start()
+                if p > 0:
+                    g_copy(p - 1, k).wait_send()
+                g_copy(p, k).start()
 
             return inner
 
         lax.fori_loop(1, side + 1, for_line, 0)
-        grad_in[j, own] = grad_send[j, own]
-        return carry
-
-    lax.fori_loop(0, 2, grad_part, 0)
+        grad_in[own, :, cut(p)] = grad_send[own, :, cut(p)]
 
     def chunk(k):
-        return (k % 2, pl.ds(pl.multiple_of((k // 2) * chunk_rows, 16), chunk_rows))
-
-    def z_copy(k, source):
-        return pltpu.make_async_remote_copy(
-            src_ref=z_out.at[chunk(k)],
-            dst_ref=z_in.at[source],
-            send_sem=z_send.at[k],
-            recv_sem=z_recv.at[source],
+        return (
+            pl.ds(pl.multiple_of((k // 2) * chunk_rows, 16), chunk_rows),
+            pl.ds(pl.multiple_of((k % 2) * chunk_cols, 128), chunk_cols),
+        )
+
+    def z_copy(p, k, source):
+        inner = pl.ds(starts[p] % chunk_cols, sizes[p])
+        return pltpu.make_async_remote_copy(
+            src_ref=z_out.at[pl.ds(pl.multiple_of((k // 2) * chunk_rows, 16), chunk_rows), cut(p)],
+            dst_ref=z_in.at[source, :, inner],
+            send_sem=z_send.at[p, k],
+            recv_sem=z_recv.at[p % 2, source],
             device_id={"dp": k * 2 + c},
             device_id_type=MESH,
         )
@@ -655,48 +761,48 @@
 
         lax.fori_loop(1, n_z, one, 0)
 
-    def to_owners(j, carry):
-        for i in range(1, side):
-            k = (own + i) % side
-            pltpu.make_async_remote_copy(
-                src_ref=grad_send.at[j, k],
-                dst_ref=grad_in.at[j, k],
-                send_sem=g_send.at[j, k],
-                recv_sem=g_recv.at[j, k],
-                device_id={"tensor": line(c, k)},
-                device_id_type=MESH,
-            ).wait_recv()
-        total = grad_in[j, 0].astype(F32)
-        for k in range(1, side):
-            total = total + grad_in[j, k].astype(F32)
-        z_out[j] = total.astype(LOW)
-
+    def z_part(p, step):
         def one(i, inner):
             k = (z + i) % n_z
 
-            @pl.when(k % 2 == j)
+            @pl.when(k % 2 == p // 2)
             def _():
-                z_copy(k, z).start()
+                step(k)
 
             return inner
 
         lax.fori_loop(1, n_z, one, 0)
-        return carry
-
-    lax.fori_loop(0, 2, to_owners, 0)
-
-    project(0)
+
+    def to_owners(p):
+        for i in range(1, side):
+            g_arrival(p, (own + i) % side).wait_recv()
+        total = grad_in[0, :, cut(p)].astype(F32)
+        for k in range(1, side):
+            total = total + grad_in[k, :, cut(p)].astype(F32)
+        z_out[:, cut(p)] = total.astype(LOW)
+        z_part(p, lambda k: z_copy(p, k, z).start())
+
+    grad_part(0)
+    grad_part(1)
+    to_owners(0)
+    grad_part(2)
+    to_owners(1)
+    grad_part(3)
+    to_owners(2)
+    to_owners(3)
 
     z_in[z] = z_out[chunk(z)]
-    z_loop(lambda k: z_copy(k, k).wait_recv())
+    z_loop(lambda k: z_copy(0, k, k).wait_recv())
+    z_loop(lambda k: z_copy(1, k, k).wait_recv())
     total = z_in[0].astype(F32)
     for k in range(1, n_z):
         total = total + z_in[k].astype(F32)
     final[(c,) + chunk(z)] = (total * (1.0 / (2 * n_z))).astype(LOW)
     z_loop(lambda k: c_copy(k, z).start())
+    project(0)
     gathered(0)
-    image_out[:, 0:half] = collect(0, 0, 0).astype(LOW)
-    image_out[:, half:width] = collect(1, 0, skip).astype(LOW)
+    image_out[:, 0:half] = collect(0, 0, 0, half).astype(LOW)
+    image_out[:, half:width] = collect(0, 1, skip, half).astype(LOW)
     z_loop(lambda k: c_copy(k, k).wait_recv())
 
     def s_copy(which):
@@ -713,16 +819,15 @@
 
     ring(lambda t: in_copy(1, t).wait_send())
     ring(lambda t: in_copy(2, t).wait_send())
-    x_loop(lambda k, other: x_copy(k, z, other).wait_send())
+    x_sent()
     for i in range(1, side):
         w_copy((place(c) + i) % side).wait_send()
         for o in range(2):
             for s in range(slots):
-                p_copy(s, o, (place(o) + i) % side).wait_send()
-            for j in range(2):
-                u_copy(o, j, (place(1 - o) + i) % side).wait_send()
-        for j in range(2):
-            g_copy(j, (place(c) + i) % side).wait_send()
+                for q in range(side if o == 0 else 1):
+                    p_copy(s, o, (place(o) + i) % side, q).wait_send()
+            u_copy(o, 3, (place(1 - o) + i) % side).wait_send()
+        g_copy(3, (place(c) + i) % side).wait_send()
 
     def r_sent(n, carry):
         o = n % 2
@@ -734,15 +839,16 @@
     lax.fori_loop(0, 2 * steps, r_sent, 0)
     for k in range(side):
         f_copy(k).wait_send()
-        for j in range(2):
-            t_copy(j, k).wait_send()
+        for p in range(4):
+            t_copy(p, k).wait_send()
 
     def q_sent(i, carry):
         q_copy((me + i) % n_t).wait_send()
         return carry
 
     lax.fori_loop(1, n_t, q_sent, 0)
-    z_loop(lambda k: z_copy(k, z).wait_send())
+    for p in range(4):
+        z_part(p, lambda k, p=p: z_copy(p, k, z).wait_send())
     z_loop(lambda k: c_copy(k, z).wait_send())
     s_copy(c).wait_send()
     s_copy(1 - c).wait_recv()
@@ -770,12 +876,15 @@
         out_shape=(
             jax.ShapeDtypeStruct((rows, width), LOW),
             jax.ShapeDtypeStruct((rows, width), LOW),
-            jax.ShapeDtypeStruct((2, 2, 192, half // 2), LOW),
+            jax.ShapeDtypeStruct((2, 192, half), LOW),
         ),
-        in_specs=[pl.BlockSpec(memory_space=pltpu.SMEM), vmem, vmem, vmem, hbm, hbm],
+        in_specs=[pl.BlockSpec(memory_space=pltpu.SMEM)] + [hbm] * 5,
         out_specs=(vmem, vmem, vmem),
         scratch_shapes=[
             pltpu.VMEM((rows, width), LOW),
+            pltpu.VMEM((3, rows, width), LOW),
+            pltpu.VMEM((3, rows, width), LOW),
+            pltpu.VMEM((slots, txt_len, 256), LOW),
             pltpu.VMEM((6, width // 128, rows, 128), LOW),
             pltpu.VMEM((slots, n_t, rows, 384), LOW),
             pltpu.VMEM((slots, n_t, rows, 384), LOW),
@@ -792,37 +901,37 @@
             pltpu.VMEM((rows, width), F32),
             pltpu.VMEM((n_t, 8, 128), F32),
             pltpu.VMEM((rows, width), LOW),
-            pltpu.VMEM((2, 2, side * rows, half // 2), LOW),
-            pltpu.VMEM((2, side, 192, half // 2), LOW),
-            pltpu.VMEM((2, side, 192, half // 2), LOW),
-            pltpu.VMEM((2, side, 192, half // 2), LOW),
-            pltpu.VMEM((2, side, 192, half // 2), LOW),
-            pltpu.VMEM((2, 192, half // 2), LOW),
+            pltpu.VMEM((2, side * rows, half), LOW),
+            pltpu.VMEM((side, 192, half), LOW),
+            pltpu.VMEM((side, 192, half), LOW),
+            pltpu.VMEM((side, 192, half), LOW),
+            pltpu.VMEM((side, 192, half), LOW),
+            pltpu.VMEM((192, half), LOW),
             pltpu.VMEM((n_z, 2 * 192 // n_z, half // 2), LOW),
-            pltpu.VMEM((2, 2, 192, half // 2), LOW),
+            pltpu.VMEM((2, 192, half), LOW),
             dma((slots, n_t)),
             dma((slots, n_t)),
             dma((side,)),
             dma((side,)),
-            dma((side, n_z)),
+            dma((side, 2, n_z // 2)),
             dma((side, n_z)),
             dma((side,)),
             dma((side,)),
-            dma((2 + slots,)),
-            dma((2, slots, side)),
-            dma((2, slots, side)),
+            dma((9 + slots,)),
+            dma((2, slots, side, side)),
+            dma((2, slots, side, side)),
             dma((2, 2, steps, side)),
             dma((2, 2, steps, side)),
             dma((n_t,)),
             dma((n_t,)),
-            dma((2, 2, side)),
-            dma((2, 2, side)),
-            dma((2, side)),
-            dma((2, side)),
-            dma((2, side)),
-            dma((2, side)),
-            dma((n_z,)),
-            dma((n_z,)),
+            dma((2, 4, side)),
+            dma((2, 4, side)),
+            dma((4, side)),
+            dma((4, side)),
+            dma((4, side)),
+            dma((4, side)),
+            dma((4, n_z)),
+            dma((2, n_z)),
             dma((n_z,)),
             dma((n_z,)),
             dma,
@@ -839,22 +948,23 @@
         out_weight,
         cotangent[0],
     )
-    parts = 4
-    by_rows = pl.BlockSpec((rows // parts, width), lambda i: (i, 0))
     return pl.pallas_call(
         finish,
-        grid=(parts,),
         out_shape=(
             jax.ShapeDtypeStruct((rows, width), LOW),
             jax.ShapeDtypeStruct((rows, width), LOW),
             jax.ShapeDtypeStruct((slots * 64, width), F32),
         ),
-        in_specs=[
-            by_rows,
-            by_rows,
-            pl.BlockSpec((2, 2, 192 // parts, half // 2), lambda i: (0, 0, i, 0)),
+        in_specs=[hbm, hbm, hbm],
+        out_specs=(hbm, hbm, hbm),
+        scratch_shapes=[
+            pltpu.VMEM((2, rows, width), LOW),
+            pltpu.VMEM((2, 192, half), LOW),
+            pltpu.VMEM((192, width), F32),
+            dma((4,)),
+            dma((4,)),
+            dma((4,)),
         ],
-        out_specs=(by_rows, by_rows, pl.BlockSpec((192 // parts, width), lambda i: (i, 0))),
     )(image, tangent, grad)
 
 

time: 132 us -> 126 us (0.955)
  Pallas kernels: 131 us -> 126 us
    pallas_call x1, Pallas kernels: 127 us -> 123 us  [on_device(): pl.pallas_call(functools.partial(body, dims), out_shape=(jax.ShapeDtypeSt...]
where the time goes in v3:
time: 126 us
  Pallas kernels  126 us (100%)
    pallas_call x1, Pallas kernels, on_device(): pl.pallas_call(functools.partial(body, dims), out_shape=(jax.ShapeDtypeSt...  123 us

profile of v3, /device:TPU:1, one launch (start us, length us, event | category | flops | bytes accessed | tf_op | source)
XLA Modules:
  0.0 126.2 jit_solution(16750716311213610556)
XLA Ops:
  0.6 123.0 %shard_map.85 = (bf16[64,2432]{1,0:T(8,128)(2,1)}, bf16[64,2432]{1,0:T(8,128)(2,1)}, bf16[2,192,1280]{2,1,0:T(8,128)(2,1)}) custom-call(s32[3,16]{1,0:T(4,128)} %bitcast.15, bf16[3,64,2432]{2,1,0:T(8,128)(2,1)} %bitcast.11, bf16[3,64,2432]{2,1,0:T(8,128)(2,1)} %bitcast.12, bf16[3,333,256]{2,1,0:T(8,128)(2,1)} %bitcast.13, bf16[192,2432]{1,0:T(8,128)(2,1)} %weight.1, ...), custom_call_target="tpu_custom_call" | custom-call | tf_op jit(solution)/shard_map/pallas_call | solution.py:874
  123.7 2.5 %shard_map.86 = (bf16[64,2432]{1,0:T(8,128)(2,1)}, bf16[64,2432]{1,0:T(8,128)(2,1)}, f32[192,2432]{1,0:T(8,128)}) custom-call(bf16[64,2432]{1,0:T(8,128)(2,1)} %get-tuple-element.9.image, bf16[64,2432]{1,0:T(8,128)(2,1)} %get-tuple-element.10.tangent, bf16[2,192,1280]{2,1,0:T(8,128)(2,1)} %get-tuple-element.11.grad), custom_call_target="tpu_custom_call" | custom-call | tf_op jit(solution)/shard_map/pallas_call | solution.py:951

commit v4 on v3

--- a/solution.py
+++ b/solution.py
@@ -90,15 +90,21 @@
     part_in,
     tan_sum,
     squares,
-    upstream,
-    up_all,
-    twin_out,
-    twin_in,
-    grad_send,
-    grad_in,
-    z_out,
-    z_in,
-    final,
+    upstream_a,
+    upstream_b,
+    up_all_a,
+    up_all_b,
+    prim_in,
+    grad_send_a,
+    grad_send_b,
+    grad_in_a,
+    grad_in_b,
+    z_out_a,
+    z_out_b,
+    z_in_a,
+    z_in_b,
+    final_a,
+    final_b,
     a_send,
     a_recv,
     w_send,
@@ -134,6 +140,13 @@
     y = me % side
     z = dp // 2
     c = dp % 2
+    upstream = (upstream_a, upstream_b)
+    up_all = (up_all_a, up_all_b)
+    grad_send = (grad_send_a, grad_send_b)
+    grad_in = (grad_in_a, grad_in_b)
+    z_out = (z_out_a, z_out_b)
+    z_in = (z_in_a, z_in_b)
+    final = (final_a, final_b)
     img = n_t * rows
     group_rows = side * rows
 
@@ -177,6 +190,14 @@
 
     lax.fori_loop(1, n_z, greet_z, 0)
     pl.semaphore_signal(barrier, inc=1, device_id=twin(), device_id_type=MESH)
+    for o in range(2):
+        for i in range(1, side):
+            pl.semaphore_signal(
+                barrier,
+                inc=1,
+                device_id={"tensor": line(o, (place(o) + i) % side), "dp": z * 2 + (1 - c)},
+                device_id_type=MESH,
+            )
 
     for o in range(2):
         for k in range(side):
@@ -218,7 +239,7 @@
         outbox[s, t, :, 128:256] = pair(1, 4)
         outbox[s, t, :, 256:384] = pair(2, 5)
 
-    pl.semaphore_wait(barrier, n_t + n_z - 1)
+    pl.semaphore_wait(barrier, n_t + n_z - 1 + 2 * (side - 1))
 
     def in_copy(s, t):
         return pltpu.make_async_remote_copy(
@@ -473,11 +494,13 @@
 
     lax.fori_loop(0, slots, one_slot, 0)
 
+    steps = 2
+    wide = half // steps
+
     def r_copy(kind, o, j, k):
-        span = pl.ds(pl.multiple_of(j * 256, 256), 256)
-        return pltpu.make_async_remote_copy(
-            src_ref=part_out.at[kind, o, k, :, span],
-            dst_ref=part_in.at[kind, o, place(1 - o), :, span],
+        return pltpu.make_async_remote_copy(
+            src_ref=part_out.at[kind, o, j, k],
+            dst_ref=part_in.at[kind, o, j, place(1 - o)],
             send_sem=r_send.at[kind, o, j, k],
             recv_sem=r_recv.at[kind, o, j, place(1 - o)],
             device_id={"tensor": line(1 - o, k)},
@@ -485,10 +508,9 @@
         )
 
     def r_arrival(kind, o, j, k):
-        span = pl.ds(pl.multiple_of(j * 256, 256), 256)
-        return pltpu.make_async_remote_copy(
-            src_ref=part_out.at[kind, o, k, :, span],
-            dst_ref=part_in.at[kind, o, k, :, span],
+        return pltpu.make_async_remote_copy(
+            src_ref=part_out.at[kind, o, j, k],
+            dst_ref=part_in.at[kind, o, j, k],
             send_sem=r_send.at[kind, o, j, k],
             recv_sem=r_recv.at[kind, o, j, k],
             device_id={"tensor": line(1 - o, k)},
@@ -518,22 +540,20 @@
     for k in range(side):
         f_arrival(k).wait_recv()
 
-    steps = half // 256
-
     def project(kind):
         def one(n, carry):
             o = n % 2
             j = n // 2
-            span = pl.ds(pl.multiple_of(j * 256, 256), 256)
+            span = pl.ds(pl.multiple_of(j * wide, 128), wide)
             part = jnp.dot(
                 proj_lhs[kind, o], group_weight[o, :, span], preferred_element_type=F32
             ).astype(LOW)
             for k in range(side):
-                part_out[kind, o, k, :, span] = part[k * rows : (k + 1) * rows]
+                part_out[kind, o, j, k] = part[k * rows : (k + 1) * rows]
             own = place(1 - o)
             for i in range(1, side):
                 r_copy(kind, o, j, (own + i) % side).start()
-            part_in[kind, o, own, :, span] = part_out[kind, o, own, :, span]
+            part_in[kind, o, j, own] = part_out[kind, o, j, own]
             return carry
 
         lax.fori_loop(0, 2 * steps, one, 0)
@@ -567,20 +587,31 @@
 
     skip = 2 * half - width
 
-    def collect(kind, o, first, last):
-        total = part_in[kind, o, 0, :, first:last].astype(F32)
+    def collect(kind, o, j, skipped):
+        total = part_in[kind, o, j, 0, :, skipped:].astype(F32)
         for k in range(1, side):
-            total = total + part_in[kind, o, k, :, first:last].astype(F32)
+            total = total + part_in[kind, o, j, k, :, skipped:].astype(F32)
         return total
 
+    def t_copy():
+        return pltpu.make_async_remote_copy(
+            src_ref=prim_t.at[1 - c],
+            dst_ref=prim_in,
+            send_sem=t_send,
+            recv_sem=t_recv,
+            device_id=twin(),
+            device_id_type=MESH,
+        )
+
+    t_copy().start()
     own_squares = jnp.zeros((1, 128), F32)
     for n in range(2 * steps):
         o, j = n % 2, n // 2
         for i in range(1, side):
             r_arrival(1, o, j, (place(1 - o) + i) % side).wait_recv()
-        first = max(j * 256, skip * o)
-        columns = collect(1, o, first, j * 256 + 256)
-        at = o * offset + first
+        skipped = skip if (o, j) == (1, 0) else 0
+        columns = collect(1, o, j, skipped)
+        at = o * offset + j * wide + skipped
         tan_sum[:, at : at + columns.shape[1]] = columns
         column_squares = jnp.sum(columns * columns, axis=0, keepdims=True)
         for lane in range(0, columns.shape[1], 128):
@@ -620,61 +651,65 @@
     normal = (tan_sum[...] / divisor).astype(LOW)
     tangent_out[...] = normal
     cot_copy.wait()
-    upstream[...] = (cot_local[...].astype(F32) - normal.astype(F32)).astype(LOW)
+    up_rows = (cot_local[...].astype(F32) - normal.astype(F32)).astype(LOW)
 
     starts = (0, 384, 640, 1024)
     sizes = (384, 256, 384, 256)
 
-    def cut(p):
-        return pl.ds(starts[p], sizes[p])
+    def of(pair, p):
+        return pair[p % 2].at[p // 2]
+
+    for p in range(4):
+        for o in range(2):
+            at = o * offset + starts[p]
+            of(upstream, p)[o] = up_rows[:, at : at + sizes[p]]
 
     def u_copy(o, p, k):
         return pltpu.make_async_remote_copy(
-            src_ref=upstream.at[:, pl.ds(o * offset + starts[p], sizes[p])],
-            dst_ref=up_all.at[o, pl.ds(place(1 - o) * rows, rows), cut(p)],
+            src_ref=of(upstream, p).at[o],
+            dst_ref=of(up_all, p).at[c, pl.ds(place(1 - o) * rows, rows)],
             send_sem=u_send.at[o, p, k],
-            recv_sem=u_recv.at[o, p, place(1 - o)],
-            device_id={"tensor": line(1 - o, k)},
-            device_id_type=MESH,
-        )
-
-    def u_arrival(o, p, k):
-        return pltpu.make_async_remote_copy(
-            src_ref=up_all.at[o, pl.ds(k * rows, rows), cut(p)],
-            dst_ref=up_all.at[o, pl.ds(k * rows, rows), cut(p)],
-            send_sem=u_send.at[o, p, k],
-            recv_sem=u_recv.at[o, p, k],
-            device_id={"tensor": line(1 - o, k)},
-            device_id_type=MESH,
-        )
+            recv_sem=u_recv.at[c, p, place(1 - o)],
+            device_id={"tensor": line(1 - o, k), "dp": z * 2 + o},
+            device_id_type=MESH,
+        )
+
+    def u_arrival(core, p, k):
+        return pltpu.make_async_remote_copy(
+            src_ref=of(upstream, p).at[c],
+            dst_ref=of(up_all, p).at[core, pl.ds(k * rows, rows)],
+            send_sem=u_send.at[c, p, k],
+            recv_sem=u_recv.at[core, p, k],
+            device_id={"tensor": line(1 - c, k), "dp": z * 2 + core},
+            device_id_type=MESH,
+        )
+
+    def up_targets(step):
+        for i in range(1, side + 1):
+            other = 1 - c
+            step(other, (place(1 - other) + i) % side)
+            if i < side:
+                step(c, (place(1 - c) + i) % side)
 
     def up_leaves(p):
-        for i in range(1, side):
-            for o in range(2):
-                k = (place(1 - o) + i) % side
-                if p > 0:
-                    u_copy(o, p - 1, k).wait_send()
-                u_copy(o, p, k).start()
+        def step(o, k):
+            if p > 1:
+                u_copy(o, p - 2, k).wait_send()
+            u_copy(o, p, k).start()
+
+        up_targets(step)
 
     up_leaves(0)
-    for o in range(2):
-        up_all[o, pl.ds(place(1 - o) * rows, rows), :] = upstream[:, o * offset : o * offset + half]
+    for p in range(4):
+        of(up_all, p)[c, pl.ds(place(1 - c) * rows, rows), :] = of(upstream, p)[c]
     up_leaves(1)
 
-    def t_copy(p, k):
-        return pltpu.make_async_remote_copy(
-            src_ref=twin_out.at[k, :, cut(p)],
-            dst_ref=twin_in.at[k, :, cut(p)],
-            send_sem=t_send.at[p, k],
-            recv_sem=t_recv.at[p, k],
-            device_id=twin(),
-            device_id_type=MESH,
-        )
+    own = place(c)
 
     def g_copy(p, k):
         return pltpu.make_async_remote_copy(
-            src_ref=grad_send.at[k, :, cut(p)],
-            dst_ref=grad_in.at[place(c), :, cut(p)],
+            src_ref=of(grad_send, p).at[k],
+            dst_ref=of(grad_in, p).at[place(c)],
             send_sem=g_send.at[p, k],
             recv_sem=g_recv.at[p, place(c)],
             device_id={"tensor": line(c, k)},
@@ -683,74 +718,71 @@
 
     def g_arrival(p, k):
         return pltpu.make_async_remote_copy(
-            src_ref=grad_in.at[k, :, cut(p)],
-            dst_ref=grad_in.at[k, :, cut(p)],
+            src_ref=of(grad_in, p).at[k],
+            dst_ref=of(grad_in, p).at[k],
             send_sem=g_send.at[p, k],
             recv_sem=g_recv.at[p, k],
             device_id={"tensor": line(c, k)},
             device_id_type=MESH,
         )
 
-    own = place(c)
-
-    def grad_part(p):
-        for o in range(2):
-            for i in range(1, side):
-                u_arrival(o, p, (place(1 - o) + i) % side).wait_recv()
+    def product(left, core, p):
+        return jnp.dot(
+            left.reshape(side * 192, group_rows),
+            of(up_all, p)[core],
+            preferred_element_type=F32,
+        )
+
+    def line_part(p):
+        for i in range(1, side):
+            u_arrival(c, p, (place(1 - c) + i) % side).wait_recv()
+        for k in range(side):
+            u_arrival(1 - c, p, k).wait_recv()
         if p + 2 < 4:
             up_leaves(p + 2)
-
-        def for_twin(i, inner):
+        both_cores = product(prim_t[c], c, p) + product(prim_in[...], 1 - c, p)
+        of(grad_send, p)[...] = both_cores.astype(LOW).reshape(side, 192, sizes[p])
+        for i in range(1, side):
             k = (own + i) % side
-            twin_out[k, :, cut(p)] = jnp.dot(
-                prim_t[1 - c, k], up_all[1 - c, :, cut(p)], preferred_element_type=F32
-            ).astype(LOW)
-            t_copy(p, k).start()
-            return inner
-
-        lax.fori_loop(1, side + 1, for_twin, 0)
-
-        def for_line(i, inner):
-            k = (own + i) % side
-            mine = jnp.dot(prim_t[c, k], up_all[c, :, cut(p)], preferred_element_type=F32)
-            t_copy(p, k).wait_recv()
-            grad_send[k, :, cut(p)] = (mine + twin_in[k, :, cut(p)].astype(F32)).astype(LOW)
-
-            @pl.when(i < side)
-            def _():
-                if p > 0:
-                    g_copy(p - 1, k).wait_send()
-                g_copy(p, k).start()
-
-            return inner
-
-        lax.fori_loop(1, side + 1, for_line, 0)
-        grad_in[own, :, cut(p)] = grad_send[own, :, cut(p)]
-
-    def chunk(k):
-        return (
-            pl.ds(pl.multiple_of((k // 2) * chunk_rows, 16), chunk_rows),
-            pl.ds(pl.multiple_of((k % 2) * chunk_cols, 128), chunk_cols),
-        )
+            if p > 1:
+                g_copy(p - 2, k).wait_send()
+            g_copy(p, k).start()
+        of(grad_in, p)[own] = of(grad_send, p)[own]
+
+    def owned(k):
+        return pl.ds(pl.multiple_of((k // 2) * chunk_rows, 16), chunk_rows)
 
     def z_copy(p, k, source):
-        inner = pl.ds(starts[p] % chunk_cols, sizes[p])
-        return pltpu.make_async_remote_copy(
-            src_ref=z_out.at[pl.ds(pl.multiple_of((k // 2) * chunk_rows, 16), chunk_rows), cut(p)],
-            dst_ref=z_in.at[source, :, inner],
+        return pltpu.make_async_remote_copy(
+            src_ref=of(z_out, p).at[owned(k)],
+            dst_ref=z_in[p % 2].at[source],
             send_sem=z_send.at[p, k],
             recv_sem=z_recv.at[p % 2, source],
             device_id={"dp": k * 2 + c},
             device_id_type=MESH,
         )
 
-    def c_copy(k, owner):
-        return pltpu.make_async_remote_copy(
-            src_ref=final.at[(c,) + chunk(owner)],
-            dst_ref=final.at[(c,) + chunk(owner)],
-            send_sem=c_send.at[k],
-            recv_sem=c_recv.at[owner],
-            device_id={"dp": k * 2 + c},
+    def c_place(way, hop):
+        return (z - (1 - 2 * way) * (1 - 2 * c) * hop + n_z) % n_z
+
+    def c_copy(way, hop, piece):
+        at = c_place(way, hop)
+        return pltpu.make_async_remote_copy(
+            src_ref=final[piece].at[c, at % 2, owned(at)],
+            dst_ref=final[piece].at[c, at % 2, owned(at)],
+            send_sem=c_send.at[way, hop % (n_z // 2), piece],
+            recv_sem=c_recv.at[at, piece],
+            device_id={"dp": c_place(way, -1) * 2 + c},
+            device_id_type=MESH,
+        )
+
+    def s_copy(which, at, piece):
+        return pltpu.make_async_remote_copy(
+            src_ref=final[piece].at[which, at % 2, owned(at)],
+            dst_ref=final[piece].at[which, at % 2, owned(at)],
+            send_sem=s_send.at[at, piece],
+            recv_sem=s_recv.at[at, piece],
+            device_id=twin(),
             device_id_type=MESH,
         )
 
@@ -776,46 +808,49 @@
     def to_owners(p):
         for i in range(1, side):
             g_arrival(p, (own + i) % side).wait_recv()
-        total = grad_in[0, :, cut(p)].astype(F32)
+        total = of(grad_in, p)[0].astype(F32)
         for k in range(1, side):
-            total = total + grad_in[k, :, cut(p)].astype(F32)
-        z_out[:, cut(p)] = total.astype(LOW)
+            total = total + of(grad_in, p)[k].astype(F32)
+        of(z_out, p)[...] = total.astype(LOW)
         z_part(p, lambda k: z_copy(p, k, z).start())
 
-    grad_part(0)
-    grad_part(1)
+    t_copy().wait_recv()
+    line_part(0)
+    line_part(1)
     to_owners(0)
-    grad_part(2)
+    line_part(2)
     to_owners(1)
-    grad_part(3)
+    line_part(3)
     to_owners(2)
     to_owners(3)
 
-    z_in[z] = z_out[chunk(z)]
-    z_loop(lambda k: z_copy(0, k, k).wait_recv())
-    z_loop(lambda k: z_copy(1, k, k).wait_recv())
-    total = z_in[0].astype(F32)
-    for k in range(1, n_z):
-        total = total + z_in[k].astype(F32)
-    final[(c,) + chunk(z)] = (total * (1.0 / (2 * n_z))).astype(LOW)
-    z_loop(lambda k: c_copy(k, z).start())
     project(0)
-    gathered(0)
-    image_out[:, 0:half] = collect(0, 0, 0, half).astype(LOW)
-    image_out[:, half:width] = collect(0, 1, skip, half).astype(LOW)
-    z_loop(lambda k: c_copy(k, k).wait_recv())
-
-    def s_copy(which):
-        return pltpu.make_async_remote_copy(
-            src_ref=final.at[which],
-            dst_ref=final.at[which],
-            send_sem=s_send,
-            recv_sem=s_recv,
-            device_id=twin(),
-            device_id_type=MESH,
-        )
-
-    s_copy(c).start()
+
+    for piece in range(2):
+        z_in[piece][z] = z_out[piece][z % 2, owned(z), :]
+        z_loop(lambda k, piece=piece: z_copy(piece, k, k).wait_recv())
+        total = z_in[piece][0].astype(F32)
+        for k in range(1, n_z):
+            total = total + z_in[piece][k].astype(F32)
+        final[piece][c, z % 2, owned(z), :] = (total * (1.0 / (2 * n_z))).astype(LOW)
+        c_copy(0, 0, piece).start()
+        c_copy(1, 0, piece).start()
+        s_copy(c, z, piece).start()
+    for hop in range(1, reach[0] + 1):
+        if hop == reach[0]:
+            gathered(0)
+            for o in range(2):
+                for j in range(steps):
+                    skipped = skip if (o, j) == (1, 0) else 0
+                    at = o * offset + j * wide + skipped
+                    image_out[:, at : at + wide - skipped] = collect(0, o, j, skipped).astype(LOW)
+        for piece in range(2):
+            for way in range(2):
+                if hop <= reach[way]:
+                    c_copy(way, hop, piece).wait_recv()
+                    if hop < reach[way]:
+                        c_copy(way, hop, piece).start()
+                    s_copy(c, c_place(way, hop), piece).start()
 
     ring(lambda t: in_copy(1, t).wait_send())
     ring(lambda t: in_copy(2, t).wait_send())
@@ -826,8 +861,8 @@
             for s in range(slots):
                 for q in range(side if o == 0 else 1):
                     p_copy(s, o, (place(o) + i) % side, q).wait_send()
-            u_copy(o, 3, (place(1 - o) + i) % side).wait_send()
-        g_copy(3, (place(c) + i) % side).wait_send()
+        for p in (2, 3):
+            g_copy(p, (place(c) + i) % side).wait_send()
 
     def r_sent(n, carry):
         o = n % 2
@@ -839,8 +874,10 @@
     lax.fori_loop(0, 2 * steps, r_sent, 0)
     for k in range(side):
         f_copy(k).wait_send()
-        for p in range(4):
-            t_copy(p, k).wait_send()
+
+    t_copy().wait_send()
+    for p in (2, 3):
+        up_targets(lambda o, k, p=p: u_copy(o, p, k).wait_send())
 
     def q_sent(i, carry):
         q_copy((me + i) % n_t).wait_send()
@@ -849,10 +886,17 @@
     lax.fori_loop(1, n_t, q_sent, 0)
     for p in range(4):
         z_part(p, lambda k, p=p: z_copy(p, k, z).wait_send())
-    z_loop(lambda k: c_copy(k, z).wait_send())
-    s_copy(c).wait_send()
-    s_copy(1 - c).wait_recv()
-    grad_out[...] = final[...]
+    for way in range(2):
+        for hop in range(reach[way]):
+            for piece in range(2):
+                c_copy(way, hop, piece).wait_send()
+    for at in range(n_z):
+        for piece in range(2):
+            s_copy(c, at, piece).wait_send()
+            s_copy(1 - c, at, piece).wait_recv()
+    for which in range(2):
+        for p in range(4):
+            grad_out[which, :, starts[p] : starts[p] + sizes[p]] = final[p % 2][which, p // 2]
 
 
 def on_device(n_t, n_dp, qkv_img, tan_img, txt_kv, head_table, out_weight, cotangent):
@@ -870,7 +914,10 @@
     dma = pltpu.SemaphoreType.DMA
     vmem = pl.BlockSpec(memory_space=pltpu.VMEM)
     hbm = pl.BlockSpec(memory_space=pl.ANY)
-    steps = half // 256
+
+    def both(*shape):
+        return [pltpu.VMEM(shape + (384,), LOW), pltpu.VMEM(shape + (256,), LOW)]
+
     image, tangent, grad = pl.pallas_call(
         functools.partial(body, dims),
         out_shape=(
@@ -896,19 +943,18 @@
             pltpu.VMEM((2, side * 256, half), LOW),
             pltpu.VMEM((2, 2, side * rows, side * 256), LOW),
             pltpu.VMEM((2, side, 192, side * rows), LOW),
-            pltpu.VMEM((2, 2, side, rows, half), LOW),
-            pltpu.VMEM((2, 2, side, rows, half), LOW),
+            pltpu.VMEM((2, 2, 2, side, rows, half // 2), LOW),
+            pltpu.VMEM((2, 2, 2, side, rows, half // 2), LOW),
             pltpu.VMEM((rows, width), F32),
             pltpu.VMEM((n_t, 8, 128), F32),
-            pltpu.VMEM((rows, width), LOW),
-            pltpu.VMEM((2, side * rows, half), LOW),
-            pltpu.VMEM((side, 192, half), LOW),
-            pltpu.VMEM((side, 192, half), LOW),
-            pltpu.VMEM((side, 192, half), LOW),
-            pltpu.VMEM((side, 192, half), LOW),
-            pltpu.VMEM((192, half), LOW),
-            pltpu.VMEM((n_z, 2 * 192 // n_z, half // 2), LOW),
-            pltpu.VMEM((2, 192, half), LOW),
+            *both(2, 2, rows),
+            *both(2, 2, side * rows),
+            pltpu.VMEM((side, 192, side * rows), LOW),
+            *both(2, side, 192),
+            *both(2, side, 192),
+            *both(2, 192),
+            *both(n_z, 2 * 192 // n_z),
+            *both(2, 2, 192),
             dma((slots, n_t)),
             dma((slots, n_t)),
             dma((side,)),
@@ -920,22 +966,22 @@
             dma((9 + slots,)),
             dma((2, slots, side, side)),
             dma((2, slots, side, side)),
-            dma((2, 2, steps, side)),
-            dma((2, 2, steps, side)),
+            dma((2, 2, 2, side)),
+            dma((2, 2, 2, side)),
             dma((n_t,)),
             dma((n_t,)),
             dma((2, 4, side)),
             dma((2, 4, side)),
-            dma((4, side)),
-            dma((4, side)),
+            dma,
+            dma,
             dma((4, side)),
             dma((4, side)),
             dma((4, n_z)),
             dma((2, n_z)),
-            dma((n_z,)),
-            dma((n_z,)),
-            dma,
-            dma,
+            dma((2, n_z // 2, 2)),
+            dma((n_z, 2)),
+            dma((n_z, 2)),
+            dma((n_z, 2)),
         ],
         compiler_params=pltpu.CompilerParams(
             collective_id=0, has_side_effects=True, vmem_limit_bytes=56 * 1024 * 1024

time: 126 us -> 125 us (level)
  Pallas kernels: 126 us -> 124 us
where the time goes in v4:
time: 125 us
  Pallas kernels  124 us (99%)
    pallas_call x1, Pallas kernels, on_device(): pl.pallas_call(functools.partial(body, dims), out_shape=(jax.ShapeDtypeSt...  122 us
    pallas_call x1, Pallas kernels, on_device(): pl.pallas_call(finish, out_shape=(jax.ShapeDtypeStruct((rows, width), LOW...  2.52 us

profile of v4, /device:TPU:1, one launch (start us, length us, event | category | flops | bytes accessed | tf_op | source)
XLA Modules:
  0.0 125.0 jit_solution(16566265011316833166)
XLA Ops:
  0.6 121.8 %shard_map.85 = (bf16[64,2432]{1,0:T(8,128)(2,1)}, bf16[64,2432]{1,0:T(8,128)(2,1)}, bf16[2,192,1280]{2,1,0:T(8,128)(2,1)}) custom-call(s32[3,16]{1,0:T(4,128)} %bitcast.15, bf16[3,64,2432]{2,1,0:T(8,128)(2,1)} %bitcast.11, bf16[3,64,2432]{2,1,0:T(8,128)(2,1)} %bitcast.12, bf16[3,333,256]{2,1,0:T(8,128)(2,1)} %bitcast.13, bf16[192,2432]{1,0:T(8,128)(2,1)} %weight.1, ...), custom_call_target="tpu_custom_call" | custom-call | tf_op jit(solution)/shard_map/pallas_call | solution.py:921
  122.5 2.5 %shard_map.86 = (bf16[64,2432]{1,0:T(8,128)(2,1)}, bf16[64,2432]{1,0:T(8,128)(2,1)}, f32[192,2432]{1,0:T(8,128)}) custom-call(bf16[64,2432]{1,0:T(8,128)(2,1)} %get-tuple-element.9.image, bf16[64,2432]{1,0:T(8,128)(2,1)} %get-tuple-element.10.tangent, bf16[2,192,1280]{2,1,0:T(8,128)(2,1)} %get-tuple-element.11.grad), custom_call_target="tpu_custom_call" | custom-call | tf_op jit(solution)/shard_map/pallas_call | solution.py:997

commit v5 on v4

--- a/solution.py
+++ b/solution.py
@@ -251,12 +251,12 @@
             device_id_type=MESH,
         )
 
-    def ring(step):
+    def ring(step, first=1, last=n_t):
         def one(i, carry):
             step(((x + i // side) % side) * side + (y + i % side) % side)
             return carry
 
-        lax.fori_loop(1, n_t, one, 0)
+        lax.fori_loop(first, last, one, 0)
 
     def in_own(s):
         return pltpu.make_async_copy(outbox.at[s, me], arrived.at[s, me], own_sem.at[1 + s])
@@ -365,11 +365,18 @@
 
         ring(one)
 
-    ring(lambda t: pick(0, t))
+    early = 6
+
+    def first_slot(t):
+        pick(0, t)
+        in_copy(0, t).start()
+
+    ring(first_slot, 1, early)
+    ring(lambda t: pick(0, t), early, n_t)
     for i in range(1, side):
         w_arrival((place(c) + i) % side).wait_recv()
     x_step(0)
-    ring(lambda t: in_copy(0, t).start())
+    ring(lambda t: in_copy(0, t).start(), early, n_t)
     depart(1)
     txt_copy.wait()
     for s in range(slots):

time: 125 us -> 124 us (level)
  no operation moved by 1% of the time
where the time goes in v5:
time: 124 us
  Pallas kernels  124 us (100%)
    pallas_call x1, Pallas kernels, on_device(): pl.pallas_call(functools.partial(body, dims), out_shape=(jax.ShapeDtypeSt...  121 us
    pallas_call x1, Pallas kernels, on_device(): pl.pallas_call(finish, out_shape=(jax.ShapeDtypeStruct((rows, width), LOW...  2.52 us

profile of v5, /device:TPU:1, one launch (start us, length us, event | category | flops | bytes accessed | tf_op | source)
XLA Modules:
  0.0 124.1 jit_solution(2429665377338014108)
XLA Ops:
  0.6 121.0 %shard_map.85 = (bf16[64,2432]{1,0:T(8,128)(2,1)}, bf16[64,2432]{1,0:T(8,128)(2,1)}, bf16[2,192,1280]{2,1,0:T(8,128)(2,1)}) custom-call(s32[3,16]{1,0:T(4,128)} %bitcast.15, bf16[3,64,2432]{2,1,0:T(8,128)(2,1)} %bitcast.11, bf16[3,64,2432]{2,1,0:T(8,128)(2,1)} %bitcast.12, bf16[3,333,256]{2,1,0:T(8,128)(2,1)} %bitcast.13, bf16[192,2432]{1,0:T(8,128)(2,1)} %weight.1, ...), custom_call_target="tpu_custom_call" | custom-call | tf_op jit(solution)/shard_map/pallas_call | solution.py:928
  121.6 2.5 %shard_map.86 = (bf16[64,2432]{1,0:T(8,128)(2,1)}, bf16[64,2432]{1,0:T(8,128)(2,1)}, f32[192,2432]{1,0:T(8,128)}) custom-call(bf16[64,2432]{1,0:T(8,128)(2,1)} %get-tuple-element.9.image, bf16[64,2432]{1,0:T(8,128)(2,1)} %get-tuple-element.10.tangent, bf16[2,192,1280]{2,1,0:T(8,128)(2,1)} %get-tuple-element.11.grad), custom_call_target="tpu_custom_call" | custom-call | tf_op jit(solution)/shard_map/pallas_call | solution.py:1004
